TPU v7x, 32 devices: a whole 2x2x4 slice. The times are simulated.
32 devices in a mesh: batch: 8 (over z, x), height: 4 (over y, core).
Axes of the slice: x: 2, y: 2, z: 4, core: 2. Of those that a mesh axis runs over, the one named last changes fastest.
Arguments:
- activations: bfloat16 [24, 32, 28, 192], P('batch', 'height'), may hold values from -6 to 6
- cotangent: bfloat16 [24, 32, 28, 192], P('batch', 'height'), may hold values from -6 to 6
- extent: int32 [24, 2], P('batch'), may hold values from 12 to 32, as said below
- inproj_weight: float32 [192, 576], P('batch'), may hold values from -0.4375 to 0.4375
- inproj_first: float32 [192, 576], P('batch'), may hold values from -48 to 48
- inproj_second: float32 [192, 576], P('batch'), may hold values from 2.688 to 21.504
- outproj_weight: float32 [192, 192], P('batch'), may hold values from -0.4375 to 0.4375
- outproj_first: float32 [192, 192], P('batch'), may hold values from -96 to 96
- outproj_second: float32 [192, 192], P('batch'), may hold values from 10.752 to 86.016
- expand_weight: float32 [192, 768], P('batch'), may hold values from -0.4375 to 0.4375
- expand_first: float32 [192, 768], P('batch'), may hold values from -24 to 24
- expand_second: float32 [192, 768], P('batch'), may hold values from 0.672 to 5.376
- reduce_weight: float32 [768, 192], P('batch'), may hold values from -0.21875 to 0.21875
- reduce_first: float32 [768, 192], P('batch'), may hold values from -48 to 48
- reduce_second: float32 [768, 192], P('batch'), may hold values from 2.688 to 21.504
- pooling_weight: float32 [3, 9, 192], replicated, may hold values from -2 to 2
- pooling_first: float32 [3, 9, 192], replicated, may hold values from -96 to 96
- pooling_second: float32 [3, 9, 192], replicated, may hold values from 10.752 to 86.016
- relheight_weight: float32 [63, 96], replicated, may hold values from -0.625 to 0.625
- relheight_first: float32 [63, 96], replicated, may hold values from -40 to 40
- relheight_second: float32 [63, 96], replicated, may hold values from 1.72032 to 13.76256
- relwidth_weight: float32 [55, 96], replicated, may hold values from -0.625 to 0.625
- relwidth_first: float32 [55, 96], replicated, may hold values from -40 to 40
- relwidth_second: float32 [55, 96], replicated, may hold values from 1.72032 to 13.76256
- gains_weight: float32 [2, 192], replicated, may hold values from 0.5 to 1.5
- gains_first: float32 [2, 192], replicated, may hold values from -96 to 96
- gains_second: float32 [2, 192], replicated, may hold values from 10.752 to 86.016
- biases_weight: float32 [2112], replicated, may hold values from -0.6 to 0.6
- biases_first: float32 [2112], replicated, may hold values from -80 to 80
- biases_second: float32 [2112], replicated, may hold values from 6.88128 to 55.05024
Outputs:
- output: bfloat16 [24, 32, 28, 192], P('batch', 'height')
- input_grad: float32 [24, 32, 28, 192], P('batch', 'height')
- inproj_new: float32 [192, 576], P('batch')
- inproj_moment: float32 [192, 576], P('batch')
- inproj_square: float32 [192, 576], P('batch')
- inproj_half: bfloat16 [192, 576], P('batch')
- outproj_new: float32 [192, 192], P('batch')
- outproj_moment: float32 [192, 192], P('batch')
- outproj_square: float32 [192, 192], P('batch')
- outproj_half: bfloat16 [192, 192], P('batch')
- expand_new: float32 [192, 768], P('batch')
- expand_moment: float32 [192, 768], P('batch')
- expand_square: float32 [192, 768], P('batch')
- expand_half: bfloat16 [192, 768], P('batch')
- reduce_new: float32 [768, 192], P('batch')
- reduce_moment: float32 [768, 192], P('batch')
- reduce_square: float32 [768, 192], P('batch')
- reduce_half: bfloat16 [768, 192], P('batch')
- pooling_new: float32 [3, 9, 192], replicated
- pooling_moment: float32 [3, 9, 192], replicated
- pooling_square: float32 [3, 9, 192], replicated
- relheight_new: float32 [63, 96], replicated
- relheight_moment: float32 [63, 96], replicated
- relheight_square: float32 [63, 96], replicated
- relwidth_new: float32 [55, 96], replicated
- relwidth_moment: float32 [55, 96], replicated
- relwidth_square: float32 [55, 96], replicated
- gains_new: float32 [2, 192], replicated
- gains_moment: float32 [2, 192], replicated
- gains_square: float32 [2, 192], replicated
- biases_new: float32 [2112], replicated
- biases_moment: float32 [2112], replicated
- biases_square: float32 [2112], replicated
Inputs may be any that keep to these rules, and one draw needn't show every extreme that they name: `extent`: column 0 is the image's valid height, at least 12, column 1 its valid width, at least 14; among the 3 images of each index of batch one has the full height 32.
All inputs are finite; a program needn't handle non-finite values.
Results may differ from a plain program's by a relative error of at most 0.012.
The roundings to bfloat16 on the way count: a program that leaves them out, or rounds other values in their place, can miss the bound.
Values may be sent and summed in bfloat16 or wider, within the bound.
A program may use at most 128 MiB of HBM per device.

v0:
```python
import jax
import jax.numpy as jnp
from jax import lax
from jax.sharding import PartitionSpec as P

STEP = 10


highest = lax.Precision.HIGHEST
norm_eps = 1e-06
beta_one = 0.9
beta_two = 0.999
adam_eps = 1e-08
masked_value = -1000000000.0
step_rates = (0.04, 0.04, 0.04, 0.04, 0.2, 0.1, 0.1, 0.5, 0.1)
decay_rates = (0.05, 0.05, 0.05, 0.05, 0.05, 0.05, 0.05, 0.0, 0.0)


def passed_along(x, axis, by):
    count = lax.axis_size(axis)
    pairs = [(i, i + by) for i in range(count) if 0 <= i + by < count]
    return lax.ppermute(x, axis, pairs)


def shortened(x):

    def short(part):
        return part.astype(jnp.bfloat16) if part.dtype == jnp.float32 else part

    return jax.tree.map(short, x)


def layer_norm(values, gain_vec, shift_vec):
    centered = values - jnp.mean(values, axis=-1, keepdims=True)
    variance = jnp.mean(centered * centered, axis=-1, keepdims=True)
    return centered * lax.rsqrt(variance + norm_eps) * gain_vec + shift_vec


def gelu_exact(values):
    return jax.nn.gelu(values, approximate=False)


def flat_dot(left_side, right_side):
    return jnp.dot(left_side, right_side, preferred_element_type=jnp.float32)


def token_dot(left_side, right_side):
    return lax.dot_general(
        left_side, right_side, (((0,), (0,)), ((), ())), preferred_element_type=jnp.float32
    )


def local_pool(query_ext, key_ext, value_ext, kernels):
    row_count = query_ext.shape[1] - 2
    col_count = query_ext.shape[2]
    widen = ((0, 0), (0, 0), (1, 1), (0, 0))
    query_pad = jnp.pad(query_ext, widen)
    key_pad = jnp.pad(key_ext, widen)
    value_pad = jnp.pad(value_ext, widen)
    query_out = 0.0
    key_out = 0.0
    value_out = 0.0
    for row_off in range(3):
        for col_off in range(3):
            tap_index = 3 * row_off + col_off
            query_out = (
                query_out
                + kernels[0, tap_index]
                * query_pad[:, row_off : row_off + row_count, col_off : col_off + col_count]
            )
            key_out = (
                key_out
                + kernels[1, tap_index]
                * key_pad[:, row_off : row_off + row_count : 2, col_off : col_off + col_count : 2]
            )
            value_out = (
                value_out
                + kernels[2, tap_index]
                * value_pad[:, row_off : row_off + row_count : 2, col_off : col_off + col_count : 2]
            )
    return (query_out, key_out, value_out)


def rel_table(pos_table, query_pos, key_count):
    distance = query_pos[:, None] - 2 * jnp.arange(key_count)[None, :] + 2 * (key_count - 1)
    onehot = (distance[:, :, None] == jnp.arange(pos_table.shape[0])[None, None, :]).astype(
        jnp.float32
    )
    return (onehot, jnp.einsum("ykj,jc->ykc", onehot, pos_table, precision=highest))


def masked_scores(query_heads, key_heads, height_half, width_half, key_mask, score_scale):
    content = jnp.einsum(
        "nyxhc,nuvhc->nhyxuv", query_heads, key_heads, preferred_element_type=jnp.float32
    )
    along_rows = jnp.einsum(
        "nyxhc,yuc->nhyxu", query_heads, height_half, preferred_element_type=jnp.float32
    )
    along_cols = jnp.einsum(
        "nyxhc,xvc->nhyxv", query_heads, width_half, preferred_element_type=jnp.float32
    )
    scores = score_scale * content + along_rows[..., None] + along_cols[..., None, :]
    scores = jnp.where(key_mask[:, None, None, None], scores, masked_value)
    return scores.reshape(scores.shape[:4] + (-1,))


def adam_step(weight, first_state, second_state, gradient, step_rate, decay_rate):
    moment = beta_one * first_state + (1.0 - beta_one) * gradient
    square = beta_two * second_state + (1.0 - beta_two) * gradient * gradient
    unbiased = moment / (1.0 - beta_one**STEP)
    scaled = square / (1.0 - beta_two**STEP)
    updated = weight * (1.0 - step_rate * decay_rate) - step_rate * unbiased / (
        jnp.sqrt(scaled) + adam_eps
    )
    return (updated, moment, square)


def shards(
    activations,
    cotangent,
    extent,
    inproj_weight,
    inproj_first,
    inproj_second,
    outproj_weight,
    outproj_first,
    outproj_second,
    expand_weight,
    expand_first,
    expand_second,
    reduce_weight,
    reduce_first,
    reduce_second,
    pooling_weight,
    pooling_first,
    pooling_second,
    relheight_weight,
    relheight_first,
    relheight_second,
    relwidth_weight,
    relwidth_first,
    relwidth_second,
    gains_weight,
    gains_first,
    gains_second,
    biases_weight,
    biases_first,
    biases_second,
):
    images, row_count, col_count, channels = activations.shape
    head_size = relheight_weight.shape[1]
    head_count = channels // head_size
    score_scale = head_size ** (-0.5)
    key_rows = row_count * lax.axis_size("height") // 2
    key_cols = col_count // 2
    token_total = images * row_count * col_count
    grid_rows = lax.axis_index("height") * row_count + jnp.arange(row_count)
    heights = extent[:, 0]
    widths = extent[:, 1]
    token_mask = (
        (grid_rows[None, :, None] < heights[:, None, None])
        & (jnp.arange(col_count)[None, None, :] < widths[:, None, None])
    ).astype(jnp.float32)
    key_mask = (2 * jnp.arange(key_rows)[None, :, None] < heights[:, None, None]) & (
        2 * jnp.arange(key_cols)[None, None, :] < widths[:, None, None]
    )
    inproj_full, outproj_full, expand_full, reduce_full = (
        lax.all_gather(inproj_weight.astype(jnp.bfloat16), "batch", axis=0, tiled=True),
        lax.all_gather(outproj_weight.astype(jnp.bfloat16), "batch", axis=0, tiled=True),
        lax.all_gather(expand_weight.astype(jnp.bfloat16), "batch", axis=0, tiled=True),
        lax.all_gather(reduce_weight.astype(jnp.bfloat16), "batch", axis=0, tiled=True),
    )
    hidden_units = expand_full.shape[1]
    first_shift = biases_weight[:channels]
    second_shift = biases_weight[channels : 2 * channels]
    inproj_bias = biases_weight[2 * channels : 5 * channels]
    outproj_bias = biases_weight[5 * channels : 6 * channels]
    expand_bias = biases_weight[6 * channels : 6 * channels + hidden_units]
    reduce_bias = biases_weight[6 * channels + hidden_units :]
    inputs = activations.astype(jnp.float32)
    normed, first_pull = jax.vjp(layer_norm, inputs, gains_weight[0], first_shift)
    normed_half = normed.astype(jnp.bfloat16).reshape(token_total, channels)
    projected = (
        flat_dot(normed_half, inproj_full).reshape(images, row_count, col_count, 3 * channels)
        + inproj_bias
    )
    projected = projected * token_mask[..., None]
    query_in = projected[..., :channels]
    key_in = projected[..., channels : 2 * channels]
    value_in = projected[..., 2 * channels :]
    rows_above = passed_along((query_in[:, -1], key_in[:, -1], value_in[:, -1]), "height", 1)
    rows_below = passed_along(query_in[:, 0].astype(jnp.bfloat16), "height", -1).astype(jnp.float32)
    query_ext = jnp.concatenate([rows_above[0][:, None], query_in, rows_below[:, None]], axis=1)
    key_ext = jnp.concatenate([rows_above[1][:, None], key_in], axis=1)
    value_ext = jnp.concatenate([rows_above[2][:, None], value_in], axis=1)
    pooled, pool_pull = jax.vjp(local_pool, query_ext, key_ext, value_ext, pooling_weight)
    query_pool, key_pool, value_pool = pooled
    query_half = query_pool.astype(jnp.bfloat16)
    key_local = key_pool.astype(jnp.bfloat16)
    value_local = value_pool.astype(jnp.bfloat16)
    key_half, value_half = (
        lax.all_gather(key_local, "height", axis=1, tiled=True),
        lax.all_gather(value_local, "height", axis=1, tiled=True),
    )
    height_hot, height_table = rel_table(relheight_weight, grid_rows, key_rows)
    width_hot, width_table = rel_table(relwidth_weight, jnp.arange(col_count), key_cols)
    height_half = height_table.astype(jnp.bfloat16)
    width_half = width_table.astype(jnp.bfloat16)
    query_heads = query_half.reshape(images, row_count, col_count, head_count, head_size)
    key_heads = key_half.reshape(images, key_rows, key_cols, head_count, head_size)
    value_keys = value_half.reshape(images, key_rows * key_cols, head_count, head_size)
    scores = masked_scores(query_heads, key_heads, height_half, width_half, key_mask, score_scale)
    peak_score = jnp.max(scores, axis=-1, keepdims=True)
    raised = jnp.exp(scores - peak_score)
    exp_total = jnp.sum(raised, axis=-1, keepdims=True)
    attn_probs = raised / exp_total
    log_total = peak_score + jnp.log(exp_total)
    attn_half = attn_probs.astype(jnp.bfloat16)
    mixed = (
        jnp.einsum(
            "nhyxk,nkhc->nyxhc", attn_half, value_keys, preferred_element_type=jnp.float32
        ).reshape(images, row_count, col_count, channels)
        + query_pool
    )
    mixed_half = mixed.astype(jnp.bfloat16).reshape(token_total, channels)
    attn_out = (
        flat_dot(mixed_half, outproj_full).reshape(images, row_count, col_count, channels)
        + outproj_bias
    )
    middle = inputs + attn_out
    second, second_pull = jax.vjp(layer_norm, middle, gains_weight[1], second_shift)
    second_half = second.astype(jnp.bfloat16).reshape(token_total, channels)
    expanded = flat_dot(second_half, expand_full) + expand_bias
    activated = gelu_exact(expanded)
    reduced = (
        flat_dot(activated.astype(jnp.bfloat16), reduce_full).reshape(
            images, row_count, col_count, channels
        )
        + reduce_bias
    )
    output = (token_mask[..., None] * (middle + reduced)).astype(jnp.bfloat16)
    upstream = cotangent.astype(jnp.float32) * token_mask[..., None]
    upstream_half = upstream.astype(jnp.bfloat16).reshape(token_total, channels)
    expanded_again = flat_dot(second_half, expand_full) + expand_bias
    activated_again, gelu_pull = jax.vjp(gelu_exact, expanded_again)
    reduce_grad = token_dot(activated_again.astype(jnp.bfloat16), upstream_half)
    reduce_bias_grad = jnp.sum(upstream_half.astype(jnp.float32), axis=0)
    (expanded_pre,) = gelu_pull(flat_dot(upstream_half, reduce_full.T))
    expanded_grad = expanded_pre.astype(jnp.bfloat16)
    expand_grad = token_dot(second_half, expanded_grad)
    expand_bias_grad = jnp.sum(expanded_grad.astype(jnp.float32), axis=0)
    second_grad = flat_dot(expanded_grad, expand_full.T).reshape(
        images, row_count, col_count, channels
    )
    middle_part, gain_two_grad, shift_two_grad = second_pull(second_grad)
    middle_grad = upstream + middle_part
    attn_grad = middle_grad.astype(jnp.bfloat16).reshape(token_total, channels)
    outproj_grad = token_dot(mixed_half, attn_grad)
    outproj_bias_grad = jnp.sum(attn_grad.astype(jnp.float32), axis=0)
    mixed_grad = (
        flat_dot(attn_grad, outproj_full.T)
        .astype(jnp.bfloat16)
        .reshape(images, row_count, col_count, head_count, head_size)
    )
    key_back_half, value_back_half = (key_half, value_half)
    key_back_heads = key_back_half.reshape(images, key_rows, key_cols, head_count, head_size)
    value_back_keys = value_back_half.reshape(images, key_rows * key_cols, head_count, head_size)
    scores_again = masked_scores(
        query_heads, key_back_heads, height_half, width_half, key_mask, score_scale
    )
    probs_again = jnp.exp(scores_again - log_total)
    prob_grad = jnp.einsum(
        "nyxhc,nkhc->nhyxk", mixed_grad, value_back_keys, preferred_element_type=jnp.float32
    )
    value_grad = jnp.einsum(
        "nhyxk,nyxhc->nkhc",
        probs_again.astype(jnp.bfloat16),
        mixed_grad,
        preferred_element_type=jnp.float32,
    )
    score_grad = probs_again * (
        prob_grad - jnp.sum(probs_again * prob_grad, axis=-1, keepdims=True)
    )
    score_half = score_grad.astype(jnp.bfloat16).reshape(
        images, head_count, row_count, col_count, key_rows, key_cols
    )
    score_wide = score_half.astype(jnp.float32)
    row_grad = jnp.sum(score_wide, axis=5)
    col_grad = jnp.sum(score_wide, axis=4)
    query_grad = score_scale * jnp.einsum(
        "nhyxuv,nuvhc->nyxhc", score_half, key_back_heads, preferred_element_type=jnp.float32
    )
    query_grad = query_grad + jnp.einsum(
        "nhyxu,yuc->nyxhc", row_grad, height_half.astype(jnp.float32), precision=highest
    )
    query_grad = query_grad + jnp.einsum(
        "nhyxv,xvc->nyxhc", col_grad, width_half.astype(jnp.float32), precision=highest
    )
    key_grad = score_scale * jnp.einsum(
        "nhyxuv,nyxhc->nuvhc", score_half, query_heads, preferred_element_type=jnp.float32
    )
    query_wide = query_half.astype(jnp.float32).reshape(
        images, row_count, col_count, head_count, head_size
    )
    height_pos_grad = jnp.einsum("nhyxu,nyxhc->yuc", row_grad, query_wide, precision=highest)
    width_pos_grad = jnp.einsum("nhyxv,nyxhc->xvc", col_grad, query_wide, precision=highest)
    relheight_grad = jnp.einsum("yuj,yuc->jc", height_hot, height_pos_grad, precision=highest)
    relwidth_grad = jnp.einsum("xvj,xvc->jc", width_hot, width_pos_grad, precision=highest)
    pool_query_grad = (query_grad + mixed_grad.astype(jnp.float32)).reshape(
        images, row_count, col_count, channels
    )
    key_share, value_share = (
        lax.psum_scatter(
            key_grad.reshape(images, key_rows, key_cols, channels).astype(jnp.bfloat16),
            "height",
            scatter_dimension=1,
            tiled=True,
        ).astype(jnp.float32),
        lax.psum_scatter(
            value_grad.reshape(images, key_rows, key_cols, channels).astype(jnp.bfloat16),
            "height",
            scatter_dimension=1,
            tiled=True,
        ).astype(jnp.float32),
    )
    query_ext_grad, key_ext_grad, value_ext_grad, pooling_grad = pool_pull(
        (pool_query_grad, key_share, value_share)
    )
    from_below = (
        passed_along(shortened(query_ext_grad[:, 0]), "height", -1),
        passed_along(key_ext_grad[:, 0].astype(jnp.bfloat16), "height", -1).astype(jnp.float32),
        passed_along(value_ext_grad[:, 0].astype(jnp.bfloat16), "height", -1).astype(jnp.float32),
    )
    from_above = passed_along(shortened(query_ext_grad[:, -1]), "height", 1)
    query_back = query_ext_grad[:, 1:-1].at[:, -1].add(from_below[0]).at[:, 0].add(from_above)
    key_back = key_ext_grad[:, 1:].at[:, -1].add(from_below[1])
    value_back = value_ext_grad[:, 1:].at[:, -1].add(from_below[2])
    proj_grad = jnp.concatenate([query_back, key_back, value_back], axis=-1) * token_mask[..., None]
    proj_half = proj_grad.astype(jnp.bfloat16).reshape(token_total, 3 * channels)
    inproj_grad = token_dot(normed_half, proj_half)
    inproj_bias_grad = jnp.sum(proj_half.astype(jnp.float32), axis=0)
    normed_grad = flat_dot(proj_half, inproj_full.T).reshape(images, row_count, col_count, channels)
    input_part, gain_one_grad, shift_one_grad = first_pull(normed_grad)
    input_grad = middle_grad + input_part
    gain_grads = jnp.stack([gain_one_grad, gain_two_grad])
    bias_grads = jnp.concatenate(
        [
            shift_one_grad,
            shift_two_grad,
            inproj_bias_grad,
            outproj_bias_grad,
            expand_bias_grad,
            reduce_bias_grad,
        ]
    )
    matrix_shards = (inproj_weight, outproj_weight, expand_weight, reduce_weight)
    summed = lax.psum(
        (
            inproj_grad,
            outproj_grad,
            expand_grad,
            reduce_grad,
            pooling_grad,
            relheight_grad,
            relwidth_grad,
            gain_grads,
            bias_grads,
        ),
        ("batch", "height"),
    )
    batch_pick = lax.axis_index("batch")
    matrix_sums = tuple(
        (
            lax.dynamic_slice_in_dim(total_grad, batch_pick * shard.shape[0], shard.shape[0], 0)
            for total_grad, shard in zip(summed[:4], matrix_shards)
        )
    )
    small_sums = summed[4:]
    gradients = tuple(matrix_sums) + tuple(small_sums)
    weights = (
        inproj_weight,
        outproj_weight,
        expand_weight,
        reduce_weight,
        pooling_weight,
        relheight_weight,
        relwidth_weight,
        gains_weight,
        biases_weight,
    )
    firsts = (
        inproj_first,
        outproj_first,
        expand_first,
        reduce_first,
        pooling_first,
        relheight_first,
        relwidth_first,
        gains_first,
        biases_first,
    )
    seconds = (
        inproj_second,
        outproj_second,
        expand_second,
        reduce_second,
        pooling_second,
        relheight_second,
        relwidth_second,
        gains_second,
        biases_second,
    )
    fresh = [
        adam_step(
            weights[index],
            firsts[index],
            seconds[index],
            gradients[index],
            step_rates[index],
            decay_rates[index],
        )
        for index in range(9)
    ]
    return (
        output,
        input_grad,
        fresh[0][0],
        fresh[0][1],
        fresh[0][2],
        fresh[0][0].astype(jnp.bfloat16),
        fresh[1][0],
        fresh[1][1],
        fresh[1][2],
        fresh[1][0].astype(jnp.bfloat16),
        fresh[2][0],
        fresh[2][1],
        fresh[2][2],
        fresh[2][0].astype(jnp.bfloat16),
        fresh[3][0],
        fresh[3][1],
        fresh[3][2],
        fresh[3][0].astype(jnp.bfloat16),
        fresh[4][0],
        fresh[4][1],
        fresh[4][2],
        fresh[5][0],
        fresh[5][1],
        fresh[5][2],
        fresh[6][0],
        fresh[6][1],
        fresh[6][2],
        fresh[7][0],
        fresh[7][1],
        fresh[7][2],
        fresh[8][0],
        fresh[8][1],
        fresh[8][2],
    )


def solution(mesh):
    in_specs = (
        P("batch", "height", None, None),
        P("batch", "height", None, None),
        P("batch", None),
        P("batch", None),
        P("batch", None),
        P("batch", None),
        P("batch", None),
        P("batch", None),
        P("batch", None),
        P("batch", None),
        P("batch", None),
        P("batch", None),
        P("batch", None),
        P("batch", None),
        P("batch", None),
        P(),
        P(),
        P(),
        P(),
        P(),
        P(),
        P(),
        P(),
        P(),
        P(),
        P(),
        P(),
        P(),
        P(),
        P(),
    )
    out_specs = (
        P("batch", "height", None, None),
        P("batch", "height", None, None),
        P("batch", None),
        P("batch", None),
        P("batch", None),
        P("batch", None),
        P("batch", None),
        P("batch", None),
        P("batch", None),
        P("batch", None),
        P("batch", None),
        P("batch", None),
        P("batch", None),
        P("batch", None),
        P("batch", None),
        P("batch", None),
        P("batch", None),
        P("batch", None),
        P(),
        P(),
        P(),
        P(),
        P(),
        P(),
        P(),
        P(),
        P(),
        P(),
        P(),
        P(),
        P(),
        P(),
        P(),
    )
    return jax.shard_map(shards, mesh=mesh, in_specs=in_specs, out_specs=out_specs, check_vma=False)
```

profile of v0, /device:TPU:0, one launch (start us, length us, event | category | flops | bytes accessed | tf_op | source)
XLA Modules:
  0.0 988.3 jit_solution(2972639871921263386)
XLA Ops:
  15.2 32.5 %all_gather.18 = bf16[192,576]{1,0:T(8,128)(2,1)S(1)} all-gather(bf16[24,576]{1,0:T(8,128)(2,1)S(1)} %convert_element_type.184), channel_id=1, replica_groups=mesh['batch'=8,'height'=4] {'batch'}, dimensions={0}, use_global_device_ids=true | all-gather | bytes 248832 | tf_op jit(solution)/shard_map/all_gather | solution.py:168
  54.0 3.7 collective-permute-start.1
  58.3 3.0 collective-permute-start
  62.0 3.0 collective-permute-start.3
  74.3 32.9 %all_gather.22 = bf16[192,768]{1,0:T(8,128)(2,1)} all-gather(bf16[24,768]{1,0:T(8,128)(2,1)S(1)} %convert_element_type.195), channel_id=1, replica_groups=mesh['batch'=8,'height'=4] {'batch'}, dimensions={0}, use_global_device_ids=true | all-gather | bytes 331776 | tf_op jit(solution)/shard_map/all_gather | solution.py:170
  107.3 33.0 %all_gather.23 = bf16[768,192]{1,0:T(8,128)(2,1)} all-gather(bf16[96,192]{1,0:T(8,128)(2,1)S(1)} %convert_element_type.197), channel_id=1, replica_groups=mesh['batch'=8,'height'=4] {'batch'}, dimensions={0}, use_global_device_ids=true | all-gather | bytes 331776 | tf_op jit(solution)/shard_map/all_gather | solution.py:171
  147.2 32.5 %all_gather.21 = bf16[192,192]{1,0:T(8,128)(2,1)} all-gather(bf16[24,192]{1,0:T(8,128)(2,1)S(1)} %copy-done.112), channel_id=1, replica_groups=mesh['batch'=8,'height'=4] {'batch'}, dimensions={0}, use_global_device_ids=true | all-gather | bytes 82944 | tf_op jit(solution)/shard_map/all_gather | solution.py:169
  182.4 12.7 %slice.432 = f32[3,4,14,192]{3,1,2,0:T(4,128)} slice(f32[3,9,30,192]{3,1,2,0:T(8,128)S(1)} %select_maximum_fusion), slice={[0:3:1], [2:9:2], [1:29:2], [0:192:1]} | slice | bytes 258048 | tf_op jit(solution)/shard_map/jvp()/slice | solution.py:74
  195.0 12.6 %slice.430 = f32[3,4,14,192]{3,1,2,0:T(4,128)} slice(f32[3,9,30,192]{3,1,2,0:T(8,128)S(1)} %select_maximum_fusion), slice={[0:3:1], [2:9:2], [0:28:2], [0:192:1]} | slice | bytes 258048 | tf_op jit(solution)/shard_map/jvp()/slice | solution.py:74
  207.6 12.6 %slice.428 = f32[3,4,14,192]{3,1,2,0:T(4,128)} slice(f32[3,9,30,192]{3,1,2,0:T(8,128)S(1)} %select_maximum_fusion), slice={[0:3:1], [1:9:2], [2:30:2], [0:192:1]} | slice | bytes 258048 | tf_op jit(solution)/shard_map/jvp()/slice | solution.py:74
  220.2 12.6 %slice.426 = f32[3,4,14,192]{3,1,2,0:T(4,128)} slice(f32[3,9,30,192]{3,1,2,0:T(8,128)S(1)} %select_maximum_fusion), slice={[0:3:1], [1:9:2], [1:29:2], [0:192:1]} | slice | bytes 258048 | tf_op jit(solution)/shard_map/jvp()/slice | solution.py:74
  232.7 12.6 %slice.424 = f32[3,4,14,192]{3,1,2,0:T(4,128)} slice(f32[3,9,30,192]{3,1,2,0:T(8,128)S(1)} %select_maximum_fusion), slice={[0:3:1], [1:9:2], [0:28:2], [0:192:1]} | slice | bytes 258048 | tf_op jit(solution)/shard_map/jvp()/slice | solution.py:74
  245.3 12.6 %slice.422 = f32[3,4,14,192]{3,1,2,0:T(4,128)} slice(f32[3,9,30,192]{3,1,2,0:T(8,128)S(1)} %select_maximum_fusion), slice={[0:3:1], [0:8:2], [2:30:2], [0:192:1]} | slice | bytes 258048 | tf_op jit(solution)/shard_map/jvp()/slice | solution.py:74
  257.9 12.6 %slice.420 = f32[3,4,14,192]{3,1,2,0:T(4,128)} slice(f32[3,9,30,192]{3,1,2,0:T(8,128)S(1)} %select_maximum_fusion), slice={[0:3:1], [0:8:2], [1:29:2], [0:192:1]} | slice | bytes 258048 | tf_op jit(solution)/shard_map/jvp()/slice | solution.py:74
  270.5 12.6 %slice.418 = f32[3,4,14,192]{3,1,2,0:T(4,128)} slice(f32[3,9,30,192]{3,1,2,0:T(8,128)S(1)} %select_maximum_fusion), slice={[0:3:1], [0:8:2], [0:28:2], [0:192:1]} | slice | bytes 258048 | tf_op jit(solution)/shard_map/jvp()/slice | solution.py:74
  283.1 12.6 %slice.434 = f32[3,4,14,192]{3,1,2,0:T(4,128)} slice(f32[3,9,30,192]{3,1,2,0:T(8,128)S(1)} %select_maximum_fusion), slice={[0:3:1], [2:9:2], [2:30:2], [0:192:1]} | slice | bytes 258048 | tf_op jit(solution)/shard_map/jvp()/slice | solution.py:74
  305.2 6.7 all_gather.20
  314.1 2.4 fusion.156
  318.8 2.8 fusion.163
  321.6 5.5 copy.441
  328.9 4.3 copy.450
  333.3 5.3 divide_convert_fusion
  339.0 6.7 all_gather.19
  346.6 2.8 fusion.20
  358.3 1.9 reshape.716
  360.2 6.1 multiply_convert_fusion
  373.9 2.1 reshape.717
  376.0 2.2 copy.449
  378.1 2.0 reshape.719
  380.2 2.3 multiply_reduce_fusion.1
  383.2 2.0 fusion.154
  395.5 9.6 multiply_convert_fusion.1
  405.1 4.3 copy.454
  409.5 3.7 fusion.47
  421.2 2.0 fusion.28
  427.8 4.5 multiply_reduce_fusion.10
  435.5 3.5 fusion.153
  445.8 3.6 collective-permute-start.5
  453.1 13.7 %all-reduce.64.cloned.1.call-done = bf16[3,16,14,192]{3,2,1,0:T(8,128)(2,1)} async-done(((bf16[3,16,14,192]{3,2,1,0:T(8,128)(2,1)}), bf16[3,16,14,192]{3,2,1,0:T(8,128)(2,1)}) %all-reduce.64.cloned.1.call-update) | async-done | bytes 258064
  471.0 14.7 %pad.203 = f32[3,9,30,192]{3,1,2,0:T(8,128)S(1)} pad(f32[3,4,14,192]{3,1,2,0:T(4,128)} %get-tuple-element.397, f32[]{:T(128)} %constant.270.clone.1), padding=0_0_0x2_0_1x0_3_1x0_0_0 | pad | bytes 751108 | tf_op jit(solution)/shard_map/transpose(jvp())/pad | solution.py:74
  485.7 19.7 %pad.204 = f32[3,9,30,192]{3,1,2,0:T(8,128)} pad(f32[3,4,14,192]{3,1,2,0:T(4,128)} %get-tuple-element.398, f32[]{:T(128)} %constant.270.clone.1), padding=0_0_0x1_1_1x2_1_1x0_0_0 | pad | bytes 751108 | tf_op jit(solution)/shard_map/transpose(jvp())/pad | solution.py:74
  505.4 19.8 %pad.205 = f32[3,9,30,192]{3,1,2,0:T(8,128)} pad(f32[3,4,14,192]{3,1,2,0:T(4,128)} %get-tuple-element.399, f32[]{:T(128)} %constant.270.clone.1), padding=0_0_0x1_1_1x1_2_1x0_0_0 | pad | bytes 751108 | tf_op jit(solution)/shard_map/transpose(jvp())/pad | solution.py:74
  525.2 19.8 %pad.206 = f32[3,9,30,192]{3,1,2,0:T(8,128)} pad(f32[3,4,14,192]{3,1,2,0:T(4,128)} %get-tuple-element.400, f32[]{:T(128)} %constant.270.clone.1), padding=0_0_0x1_1_1x0_3_1x0_0_0 | pad | bytes 751108 | tf_op jit(solution)/shard_map/transpose(jvp())/pad | solution.py:74
  545.0 19.8 %pad.207 = f32[3,9,30,192]{3,1,2,0:T(8,128)} pad(f32[3,4,14,192]{3,1,2,0:T(4,128)} %get-tuple-element.401, f32[]{:T(128)} %constant.270.clone.1), padding=0_0_0x0_2_1x2_1_1x0_0_0 | pad | bytes 751108 | tf_op jit(solution)/shard_map/transpose(jvp())/pad | solution.py:74
  564.8 19.8 %pad.208 = f32[3,9,30,192]{3,1,2,0:T(8,128)} pad(f32[3,4,14,192]{3,1,2,0:T(4,128)} %get-tuple-element.402, f32[]{:T(128)} %constant.270.clone.1), padding=0_0_0x0_2_1x1_2_1x0_0_0 | pad | bytes 751108 | tf_op jit(solution)/shard_map/transpose(jvp())/pad | solution.py:74
  584.6 13.9 %pad.209 = f32[3,9,30,192]{3,1,2,0:T(8,128)} pad(f32[3,4,14,192]{3,1,2,0:T(4,128)S(1)} %get-tuple-element.403, f32[]{:T(128)} %constant.270.clone.1), padding=0_0_0x0_2_1x0_3_1x0_0_0 | pad | bytes 751108 | tf_op jit(solution)/shard_map/transpose(jvp())/pad | solution.py:74
  598.4 13.9 %pad.201 = f32[3,9,30,192]{3,1,2,0:T(8,128)} pad(f32[3,4,14,192]{3,1,2,0:T(4,128)S(1)} %get-tuple-element.404, f32[]{:T(128)} %constant.270.clone.1), padding=0_0_0x2_0_1x2_1_1x0_0_0 | pad | bytes 751108 | tf_op jit(solution)/shard_map/transpose(jvp())/pad | solution.py:74
  612.4 5.7 add_add_fusion
  620.0 3.5 scatter-add.15
  627.8 3.5 scatter-add.16
  632.6 3.0 fusion.93
  635.6 4.4 pad.211
  640.0 4.4 pad.212
  644.4 7.0 pad.213
  651.4 4.6 pad.214
  656.1 7.0 pad.215
  663.1 7.0 pad.216
  670.1 7.0 pad.217
  677.1 7.0 pad.218
  684.0 4.6 pad.210
  688.9 3.7 add_add_fusion.3
  696.5 3.5 scatter-add.19
  710.2 122.1 %all-reduce.66.cloned.1.call-done = (f32[3,9,192]{2,0,1:T(4,128)}, f32[63,96]{1,0:T(8,128)}, f32[55,96]{1,0:T(8,128)}, f32[2,192]{1,0:T(2,128)}, f32[2112]{0:T(1024)}) async-done(((f32[3,9,192]{2,0,1:T(4,128)}, f32[63,96]{1,0:T(8,128)}, f32[55,96]{1,0:T(8,128)}, f32[2,192]{1,0:T(2,128)}, f32[2112]{0:T(1024)}), (f32[3,9,192]{2,0,1:T(4,128)}, f32[63,96]{1,0:T(8,128)}, f32[55,96]{1,0:T(8,128)}, ...) | async-done | bytes 76048 | tf_op jit(solution)/shard_map/psum | solution.py:357
  839.2 136.1 %all-reduce.68.cloned.1.call-done = (f32[192,576]{1,0:T(8,128)}, f32[192,192]{1,0:T(8,128)}, f32[192,768]{1,0:T(8,128)}, f32[768,192]{1,0:T(8,128)}) async-done(((f32[192,576]{1,0:T(8,128)}, f32[192,192]{1,0:T(8,128)}, f32[192,768]{1,0:T(8,128)}, f32[768,192]{1,0:T(8,128)}), (f32[192,576]{1,0:T(8,128)}, f32[192,192]{1,0:T(8,128)}, f32[192,768]{1,0:T(8,128)}, ...) | async-done | bytes 1769488 | tf_op jit(solution)/shard_map/psum | solution.py:357
  (620 shorter events, 141.2 us)
Async XLA Ops:
  7.2 459.5 %all-reduce.64.cloned.1.call-start = ((), (), s32[]{:S(2)}) async-start(), calls=%async_computation.2 | async-start | bytes 786432
  9.4 38.3 %copy-start.208 = (f32[192]{0:T(256)}, f32[192]{0:T(256)S(1)}, u32[]{:S(2)}) copy-start(f32[192]{0:T(256)S(1)} %get-tuple-element.435) | copy-start | bytes 2308
  12.7 35.0 %copy-start.77 = (f32[3,8,28]{2,1,0:T(8,128)}, f32[3,8,28]{2,1,0:T(8,128)S(1)}, u32[]{:S(2)}) copy-start(f32[3,8,28]{2,1,0:T(8,128)S(1)} %broadcast_multiply_fusion.10) | copy-start | bytes 8068
  14.1 33.6 %copy-start.87 = (f32[3,8,28]{2,1,0:T(8,128)}, f32[3,8,28]{2,1,0:T(8,128)S(1)}, u32[]{:S(2)}) copy-start(f32[3,8,28]{2,1,0:T(8,128)S(1)} %fusion.135) | copy-start | bytes 8068
  15.2 35.9 %copy-start.70 = (f32[3,8,28]{1,2,0:T(8,128)}, f32[3,8,28]{1,2,0:T(8,128)S(1)}, u32[]{:S(2)}) copy-start(f32[3,8,28]{1,2,0:T(8,128)S(1)} %copy.423) | copy-start | bytes 8068
  50.0 19.5 %copy-start.94 = (f32[3,9,192]{2,0,1:T(4,128)S(1)}, f32[3,9,192]{2,0,1:T(4,128)}, u32[]{:S(2)}) copy-start(f32[3,9,192]{2,0,1:T(4,128)} %param.53) | copy-start | bytes 62212
  51.7 128.0 %collective-permute-start.2 = (bf16[3,28,192]{2,1,0:T(8,128)(2,1)}, bf16[3,28,192]{2,1,0:T(8,128)(2,1)}, u32[]{:S(2)}, u32[]{:S(2)}) collective-permute-start(bf16[3,28,192]{2,1,0:T(8,128)(2,1)} %bitcast.227), channel_id=1, source_target_pairs={{1,0},{2,1},{3,2},{5,4},{6,5},{7,6},{9,8},{10,9},{11,10},{13,12},{... | collective-permute-start | bytes 96776 | tf_op jit(solution)/shard_map/ppermute | solution.py:22
  54.0 258.9 %collective-permute-start.1 = (f32[3,28,192]{2,1,0:T(8,128)}, f32[3,28,192]{2,1,0:T(8,128)}, u32[]{:S(2)}, u32[]{:S(2)}) collective-permute-start(f32[3,28,192]{2,1,0:T(8,128)} %bitcast.226), channel_id=1, source_target_pairs={{0,1},{1,2},{2,3},{4,5},{5,6},{6,7},{8,9},{9,10},{10,11},{12,13},{... | collective-permute-start | bytes 193544 | tf_op jit(solution)/shard_map/ppermute | solution.py:22
  58.3 237.4 %collective-permute-start = (f32[3,28,192]{2,1,0:T(8,128)}, f32[3,28,192]{2,1,0:T(8,128)}, u32[]{:S(2)}, u32[]{:S(2)}) collective-permute-start(f32[3,28,192]{2,1,0:T(8,128)} %bitcast.224), channel_id=1, source_target_pairs={{0,1},{1,2},{2,3},{4,5},{5,6},{6,7},{8,9},{9,10},{10,11},{12,13},{... | collective-permute-start | bytes 193544 | tf_op jit(solution)/shard_map/ppermute | solution.py:22
  62.0 119.2 %collective-permute-start.3 = (f32[3,28,192]{2,1,0:T(8,128)}, f32[3,28,192]{2,1,0:T(8,128)}, u32[]{:S(2)}, u32[]{:S(2)}) collective-permute-start(f32[3,28,192]{2,1,0:T(8,128)} %bitcast.225), channel_id=1, source_target_pairs={{0,1},{1,2},{2,3},{4,5},{5,6},{6,7},{8,9},{9,10},{10,11},{12,13},{... | collective-permute-start | bytes 193544 | tf_op jit(solution)/shard_map/ppermute | solution.py:22
  70.8 69.5 %copy-start.17 = (bf16[3,8,28,192]{3,1,2,0:T(8,128)(2,1)S(1)}, bf16[3,8,28,192]{3,1,2,0:T(8,128)(2,1)}, u32[]{:S(2)}) copy-start(bf16[3,8,28,192]{3,1,2,0:T(8,128)(2,1)} %param.39) | copy-start | bytes 774148
  71.9 71.5 %copy-start.9 = (f32[3,8,28,192]{3,1,2,0:T(8,128)}, f32[3,8,28,192]{3,1,2,0:T(8,128)S(1)}, u32[]{:S(2)}) copy-start(f32[3,8,28,192]{3,1,2,0:T(8,128)S(1)} %get-tuple-element.371) | copy-start | bytes 1548292
  141.1 41.0 %copy-start.22 = (f32[3,8,28,192]{3,1,2,0:T(8,128)S(1)}, f32[3,8,28,192]{3,1,2,0:T(8,128)}, u32[]{:S(2)}) copy-start(f32[3,8,28,192]{3,1,2,0:T(8,128)} %get-tuple-element.370) | copy-start | bytes 1548292
  142.2 171.7 %copy-start.2 = (f32[3,8,28,192]{3,2,0,1:T(8,128)}, f32[3,8,28,192]{3,2,0,1:T(8,128)S(1)}, u32[]{:S(2)}) copy-start(f32[3,8,28,192]{3,2,0,1:T(8,128)S(1)} %copy.562) | copy-start | bytes 1548292
  297.5 41.1 %copy-start.25 = (f32[3,4,14,192]{3,2,0,1:T(8,128)}, f32[3,4,14,192]{3,2,0,1:T(8,128)S(1)}, u32[]{:S(2)}) copy-start(f32[3,4,14,192]{3,2,0,1:T(8,128)S(1)} %slice.390) | copy-start | bytes 387076
  297.7 40.9 %copy-start.27 = (f32[3,4,14,192]{3,2,0,1:T(8,128)}, f32[3,4,14,192]{3,2,0,1:T(8,128)S(1)}, u32[]{:S(2)}) copy-start(f32[3,4,14,192]{3,2,0,1:T(8,128)S(1)} %slice.388) | copy-start | bytes 387076
  297.9 40.7 %copy-start.29 = (f32[3,4,14,192]{3,2,0,1:T(8,128)}, f32[3,4,14,192]{3,2,0,1:T(8,128)S(1)}, u32[]{:S(2)}) copy-start(f32[3,4,14,192]{3,2,0,1:T(8,128)S(1)} %slice.386) | copy-start | bytes 387076
  298.1 40.5 %copy-start.31 = (f32[3,4,14,192]{3,2,0,1:T(8,128)}, f32[3,4,14,192]{3,2,0,1:T(8,128)S(1)}, u32[]{:S(2)}) copy-start(f32[3,4,14,192]{3,2,0,1:T(8,128)S(1)} %slice.384) | copy-start | bytes 387076
  433.6 198.8 %reduce-scatter.3.cloned.1.call-start = ((), (), s32[]{:S(2)}) async-start(), calls=%async_computation.1 | async-start | bytes 491520 | tf_op jit(solution)/shard_map/reduce_scatter | solution.py:319
  440.8 9.3 collective-permute-start.4
  444.6 23.0 %copy-start.46 = (f32[3,4,14,192]{3,1,2,0:T(4,128)S(1)}, f32[3,4,14,192]{3,1,2,0:T(4,128)}, u32[]{:S(2)}) copy-start(f32[3,4,14,192]{3,1,2,0:T(4,128)} %slice.432) | copy-start | bytes 387076
  444.6 23.0 %copy-start.48 = (f32[3,4,14,192]{3,1,2,0:T(4,128)S(1)}, f32[3,4,14,192]{3,1,2,0:T(4,128)}, u32[]{:S(2)}) copy-start(f32[3,4,14,192]{3,1,2,0:T(4,128)} %slice.430) | copy-start | bytes 387076
  444.6 23.0 %copy-start.50 = (f32[3,4,14,192]{3,1,2,0:T(4,128)S(1)}, f32[3,4,14,192]{3,1,2,0:T(4,128)}, u32[]{:S(2)}) copy-start(f32[3,4,14,192]{3,1,2,0:T(4,128)} %slice.428) | copy-start | bytes 387076
  444.6 23.0 %copy-start.52 = (f32[3,4,14,192]{3,1,2,0:T(4,128)S(1)}, f32[3,4,14,192]{3,1,2,0:T(4,128)}, u32[]{:S(2)}) copy-start(f32[3,4,14,192]{3,1,2,0:T(4,128)} %slice.426) | copy-start | bytes 387076
  444.6 23.0 %copy-start.53 = (f32[3,4,14,192]{3,1,2,0:T(4,128)S(1)}, f32[3,4,14,192]{3,1,2,0:T(4,128)}, u32[]{:S(2)}) copy-start(f32[3,4,14,192]{3,1,2,0:T(4,128)} %slice.424) | copy-start | bytes 387076
  444.6 23.0 %copy-start.54 = (f32[3,4,14,192]{3,1,2,0:T(4,128)S(1)}, f32[3,4,14,192]{3,1,2,0:T(4,128)}, u32[]{:S(2)}) copy-start(f32[3,4,14,192]{3,1,2,0:T(4,128)} %slice.422) | copy-start | bytes 387076
  444.6 23.0 %copy-start.55 = (f32[3,4,14,192]{3,1,2,0:T(4,128)S(1)}, f32[3,4,14,192]{3,1,2,0:T(4,128)}, u32[]{:S(2)}) copy-start(f32[3,4,14,192]{3,1,2,0:T(4,128)} %slice.420) | copy-start | bytes 387076
  444.6 23.0 %copy-start.56 = (f32[3,4,14,192]{3,1,2,0:T(4,128)S(1)}, f32[3,4,14,192]{3,1,2,0:T(4,128)}, u32[]{:S(2)}) copy-start(f32[3,4,14,192]{3,1,2,0:T(4,128)} %slice.418) | copy-start | bytes 387076
  444.7 23.0 %copy-start.57 = (f32[3,4,14,192]{3,1,2,0:T(4,128)S(1)}, f32[3,4,14,192]{3,1,2,0:T(4,128)}, u32[]{:S(2)}) copy-start(f32[3,4,14,192]{3,1,2,0:T(4,128)} %slice.434) | copy-start | bytes 387076
  445.8 5.9 collective-permute-start.5
  449.4 19.3 %copy-start.175 = (f32[1,1,192]{2,0,1:T(1,128)S(1)}, f32[1,1,192]{2,0,1:T(1,128)}, u32[]{:S(2)}) copy-start(f32[1,1,192]{2,0,1:T(1,128)} %get-tuple-element.409) | copy-start | bytes 2308
  449.5 382.8 %all-reduce.66.cloned.1.call-start = ((), (), s32[]{:S(2)}) async-start(), calls=%async_computation.3 | async-start | bytes 225280 | tf_op jit(solution)/shard_map/psum | solution.py:357
  450.9 19.6 %copy-start.12 = (f32[3,8,28,192]{3,2,0,1:T(8,128)}, f32[3,8,28,192]{3,2,0,1:T(8,128)S(1)}, u32[]{:S(2)}) copy-start(f32[3,8,28,192]{3,2,0,1:T(8,128)S(1)} %fusion.119) | copy-start | bytes 1548292
  618.2 8.1 collective-permute-start.6
  656.1 28.0 %copy-start.68 = (f32[3,4,14,192]{3,2,0,1:T(8,128)S(1)}, f32[3,4,14,192]{3,2,0,1:T(8,128)}, u32[]{:S(2)}) copy-start(f32[3,4,14,192]{3,2,0,1:T(8,128)} %get-tuple-element.395) | copy-start | bytes 387076
  692.6 3.8 collective-permute-start.7
  707.1 268.2 %all-reduce.68.cloned.1.call-start = ((), (), s32[]{:S(2)}) async-start(), calls=%async_computation.4 | async-start | bytes 4128768 | tf_op jit(solution)/shard_map/psum | solution.py:357
  708.7 123.6 %copy-start.113 = (f32[2112]{0:T(1024)S(1)}, f32[2112]{0:T(1024)}, u32[]{:S(2)}) copy-start(f32[2112]{0:T(1024)} %param.65) | copy-start | bytes 25348
  708.7 123.6 %copy-start.126 = (f32[2112]{0:T(1024)S(1)}, f32[2112]{0:T(1024)}, u32[]{:S(2)}) copy-start(f32[2112]{0:T(1024)} %param.66) | copy-start | bytes 25348
  708.7 123.6 %copy-start.127 = (f32[2112]{0:T(1024)S(1)}, f32[2112]{0:T(1024)}, u32[]{:S(2)}) copy-start(f32[2112]{0:T(1024)} %param.67) | copy-start | bytes 25348
  708.7 125.0 %copy-start.179 = (f32[2,192]{1,0:T(2,128)S(1)}, f32[2,192]{1,0:T(2,128)}, u32[]{:S(2)}) copy-start(f32[2,192]{1,0:T(2,128)} %param.62) | copy-start | bytes 4612
  708.7 125.0 %copy-start.214 = (f32[2,192]{1,0:T(2,128)S(1)}, f32[2,192]{1,0:T(2,128)}, u32[]{:S(2)}) copy-start(f32[2,192]{1,0:T(2,128)} %param.63) | copy-start | bytes 4612
  708.7 124.9 %copy-start.215 = (f32[2,192]{1,0:T(2,128)S(1)}, f32[2,192]{1,0:T(2,128)}, u32[]{:S(2)}) copy-start(f32[2,192]{1,0:T(2,128)} %param.64) | copy-start | bytes 4612
  708.7 126.2 %copy-start.93 = (f32[55,96]{1,0:T(8,128)S(1)}, f32[55,96]{1,0:T(8,128)}, u32[]{:S(2)}) copy-start(f32[55,96]{1,0:T(8,128)} %param.59) | copy-start | bytes 63364
  708.7 126.2 %copy-start.118 = (f32[55,96]{1,0:T(8,128)S(1)}, f32[55,96]{1,0:T(8,128)}, u32[]{:S(2)}) copy-start(f32[55,96]{1,0:T(8,128)} %param.60) | copy-start | bytes 63364
  708.8 126.2 %copy-start.119 = (f32[55,96]{1,0:T(8,128)S(1)}, f32[55,96]{1,0:T(8,128)}, u32[]{:S(2)}) copy-start(f32[55,96]{1,0:T(8,128)} %param.61) | copy-start | bytes 63364
  708.8 127.6 %copy-start.91 = (f32[63,96]{1,0:T(8,128)S(1)}, f32[63,96]{1,0:T(8,128)}, u32[]{:S(2)}) copy-start(f32[63,96]{1,0:T(8,128)} %param.56) | copy-start | bytes 72580
  708.8 127.6 %copy-start.116 = (f32[63,96]{1,0:T(8,128)S(1)}, f32[63,96]{1,0:T(8,128)}, u32[]{:S(2)}) copy-start(f32[63,96]{1,0:T(8,128)} %param.57) | copy-start | bytes 72580
  708.8 127.6 %copy-start.117 = (f32[63,96]{1,0:T(8,128)S(1)}, f32[63,96]{1,0:T(8,128)}, u32[]{:S(2)}) copy-start(f32[63,96]{1,0:T(8,128)} %param.58) | copy-start | bytes 72580
  708.8 129.0 %copy-start.95 = (f32[3,9,192]{2,0,1:T(4,128)S(1)}, f32[3,9,192]{2,0,1:T(4,128)}, u32[]{:S(2)}) copy-start(f32[3,9,192]{2,0,1:T(4,128)} %param.53) | copy-start | bytes 62212
  708.8 129.0 %copy-start.114 = (f32[3,9,192]{2,0,1:T(4,128)S(1)}, f32[3,9,192]{2,0,1:T(4,128)}, u32[]{:S(2)}) copy-start(f32[3,9,192]{2,0,1:T(4,128)} %param.54) | copy-start | bytes 62212
  708.8 128.9 %copy-start.115 = (f32[3,9,192]{2,0,1:T(4,128)S(1)}, f32[3,9,192]{2,0,1:T(4,128)}, u32[]{:S(2)}) copy-start(f32[3,9,192]{2,0,1:T(4,128)} %param.55) | copy-start | bytes 62212
  708.8 266.5 %copy-start.83 = (f32[24,576]{1,0:T(8,128)S(1)}, f32[24,576]{1,0:T(8,128)}, u32[]{:S(2)}) copy-start(f32[24,576]{1,0:T(8,128)} %param.41) | copy-start | bytes 165892
  708.9 266.5 %copy-start.110 = (f32[24,576]{1,0:T(8,128)S(1)}, f32[24,576]{1,0:T(8,128)}, u32[]{:S(2)}) copy-start(f32[24,576]{1,0:T(8,128)} %param.42) | copy-start | bytes 165892
  708.9 266.5 %copy-start.111 = (f32[24,576]{1,0:T(8,128)S(1)}, f32[24,576]{1,0:T(8,128)}, u32[]{:S(2)}) copy-start(f32[24,576]{1,0:T(8,128)} %param.43) | copy-start | bytes 165892
  708.9 268.0 %copy-start.104 = (f32[24,192]{1,0:T(8,128)S(1)}, f32[24,192]{1,0:T(8,128)}, u32[]{:S(2)}) copy-start(f32[24,192]{1,0:T(8,128)} %param.44) | copy-start | bytes 55300
  708.9 268.0 %copy-start.120 = (f32[24,192]{1,0:T(8,128)S(1)}, f32[24,192]{1,0:T(8,128)}, u32[]{:S(2)}) copy-start(f32[24,192]{1,0:T(8,128)} %param.45) | copy-start | bytes 55300
  708.9 268.0 %copy-start.121 = (f32[24,192]{1,0:T(8,128)S(1)}, f32[24,192]{1,0:T(8,128)}, u32[]{:S(2)}) copy-start(f32[24,192]{1,0:T(8,128)} %param.46) | copy-start | bytes 55300
  710.2 268.1 %copy-start.82 = (f32[24,768]{1,0:T(8,128)S(1)}, f32[24,768]{1,0:T(8,128)}, u32[]{:S(2)}) copy-start(f32[24,768]{1,0:T(8,128)} %param.47) | copy-start | bytes 221188
  710.2 268.1 %copy-start.105 = (f32[24,768]{1,0:T(8,128)S(1)}, f32[24,768]{1,0:T(8,128)}, u32[]{:S(2)}) copy-start(f32[24,768]{1,0:T(8,128)} %param.48) | copy-start | bytes 221188
  710.2 268.1 %copy-start.106 = (f32[24,768]{1,0:T(8,128)S(1)}, f32[24,768]{1,0:T(8,128)}, u32[]{:S(2)}) copy-start(f32[24,768]{1,0:T(8,128)} %param.49) | copy-start | bytes 221188
  710.2 269.7 %copy-start.72 = (f32[96,192]{1,0:T(8,128)S(1)}, f32[96,192]{1,0:T(8,128)}, u32[]{:S(2)}) copy-start(f32[96,192]{1,0:T(8,128)} %param.50) | copy-start | bytes 221188
  710.2 269.7 %copy-start.101 = (f32[96,192]{1,0:T(8,128)S(1)}, f32[96,192]{1,0:T(8,128)}, u32[]{:S(2)}) copy-start(f32[96,192]{1,0:T(8,128)} %param.51) | copy-start | bytes 221188
  710.2 269.7 %copy-start.102 = (f32[96,192]{1,0:T(8,128)S(1)}, f32[96,192]{1,0:T(8,128)}, u32[]{:S(2)}) copy-start(f32[96,192]{1,0:T(8,128)} %param.52) | copy-start | bytes 221188
  (167 other events, 875.4 us)
Sparse Core Ops, SparseCore 0:
  433.7 32.9 all-reduce.63
  469.4 20.8 reduce-scatter.2
  707.2 125.0 all-reduce.65
  839.0 136.2 all-reduce.67
where the time goes:
time: 1010 us; the launch traced here: 988 us
  local copies, waits for them, and re-layouts  396 us (39%)
  waiting for transfers between devices  273 us (27%)
  blocking collectives  144 us (14%)
  other arithmetic  91.1 us (9%)
  matrix products  46.6 us (5%)
  starting transfers between devices  19.3 us (2%)
  between operations  17.7 us (2%)
    psum x2, waiting for transfers between devices, shards(): lax.psum((inproj_grad, outproj_grad, expand_grad, reduce_grad, pooling_gr...  258 us
    pad x9, local copies, waits for them, and re-layouts, local_pool(): key_pad[:, row_off:row_off + row_count:2, col_off:col_off + col_count:2]  142 us
    slice x9, local copies, waits for them, and re-layouts, local_pool(): key_pad[:, row_off:row_off + row_count:2, col_off:col_off + col_count:2]  113 us
    pad x9, local copies, waits for them, and re-layouts, local_pool(): value_pad[:, row_off:row_off + row_count:2, col_off:col_off + col_count:2]  53.1 us
    all_gather x1, blocking collectives, shards(): lax.all_gather(reduce_weight.astype(jnp.bfloat16), 'batch', axis=0, tiled...  33 us
    all_gather x1, blocking collectives, shards(): lax.all_gather(expand_weight.astype(jnp.bfloat16), 'batch', axis=0, tiled...  32.9 us
    all_gather x1, blocking collectives, shards(): lax.all_gather(outproj_weight.astype(jnp.bfloat16), 'batch', axis=0, tile...  32.5 us
    all_gather x1, blocking collectives, shards(): lax.all_gather(inproj_weight.astype(jnp.bfloat16), 'batch', axis=0, tiled...  32.5 us
  transfers between devices with their start and end apart: 12, of which 4 were waited for; matrix products, arithmetic and copies ran while one was open for 34% of the time, Pallas kernels for 0%

commit v1 on v0

v1 whole, which is shorter than its diff:
```python
import functools
import types

import jax
import jax.numpy as jnp
from jax import lax
from jax.experimental import pallas as pl
from jax.experimental.pallas import tpu as pltpu
from jax.sharding import PartitionSpec as P

STEP = 10
MESH = pl.DeviceIdType.MESH
f32 = jnp.float32
bf16 = jnp.bfloat16

norm_eps = 1e-06
beta_one = 0.9
beta_two = 0.999
adam_eps = 1e-08
masked_value = -1000000000.0
step_rates = (0.04, 0.04, 0.04, 0.04, 0.2, 0.1, 0.1, 0.5, 0.1)
decay_rates = (0.05, 0.05, 0.05, 0.05, 0.05, 0.05, 0.05, 0.0, 0.0)

IMG, R, C, D, HD, HID = 3, 8, 28, 192, 96, 768
T = R * C
TX = T + 2 * R
HG = 4
KR, KC, KCP = R * HG // 2, C // 2, 16
KL = R // 2
KEYS = KR * KCP
SCALE = HD ** (-0.5)
KROWS = (KL + 1) * KCP
HX = 32
PE = HID + 4 * D + 2 * 128
PI = 3 * D


def nn(a, b):
    return lax.dot_general(a, b, (((1,), (0,)), ((), ())), preferred_element_type=f32)


def nt(a, b):
    return lax.dot_general(a, b, (((1,), (1,)), ((), ())), preferred_element_type=f32)


def tn(a, b):
    return lax.dot_general(a, b, (((0,), (0,)), ((), ())), preferred_element_type=f32)


def iota(shape, axis):
    return lax.broadcasted_iota(jnp.int32, shape, axis)


def rolled(x, by):
    return pltpu.roll(x, by % x.shape[0], 0)


def halves(x, axis):
    high = x.astype(bf16)
    return jnp.concatenate([high, (x - high.astype(f32)).astype(bf16)], axis=axis)


def normalise(x):
    mean = jnp.sum(x, axis=1, keepdims=True) * (1.0 / D)
    centered = x - mean
    inverse = lax.rsqrt(jnp.sum(centered * centered, axis=1, keepdims=True) * (1.0 / D) + norm_eps)
    return centered * inverse, inverse


def normalise_back(grad, gain, hat, inverse):
    scaled = grad * gain
    one = jnp.sum(scaled, axis=1, keepdims=True) * (1.0 / D)
    two = jnp.sum(scaled * hat, axis=1, keepdims=True) * (1.0 / D)
    return inverse * (scaled - one - hat * two)


def folded(x):
    return jnp.sum(x.reshape(x.shape[0] // 8, 8, x.shape[1]), axis=0)


def main_kernel(B, tree, *refs):
    r = types.SimpleNamespace(**jax.tree.unflatten(tree, refs))
    me = lax.axis_index("batch")
    hh = lax.axis_index("height")
    QB = B // HG
    rows = r.w_in.shape[0]

    def loop(first, last, body):
        def step(i, carry):
            body(i)
            return carry

        lax.fori_loop(first, last, step, 0)

    def next_batch(k):
        return lax.rem(me + k, B)

    def next_height(k):
        return lax.rem(hh + k, HG)

    local = [
        (r.act, r.v_act),
        (r.w_in, r.v_in),
        (r.w_out, r.v_out),
        (r.w_exp, r.v_exp),
        (r.w_red, r.v_red),
        (r.pool, r.v_pool),
        (r.relh, r.v_relh),
        (r.relw, r.v_relw),
        (r.gains, r.v_gains),
        (r.biases, r.v_biases.at[0]),
        (r.cot, r.v_cot),
    ]
    local = [pltpu.make_async_copy(a, b, r.s_local.at[k]) for k, (a, b) in enumerate(local)]
    for copy in local:
        copy.start()

    barrier = pltpu.get_barrier_semaphore()

    def greet_batch(k):
        pl.semaphore_signal(barrier, inc=1, device_id=(next_batch(k), hh), device_id_type=MESH)

    loop(1, B, greet_batch)
    for k in range(1, HG):
        pl.semaphore_signal(barrier, inc=1, device_id=(me, next_height(k)), device_id_type=MESH)

    def to_batch(src, dst, send, recv, b):
        return pltpu.make_async_remote_copy(
            src_ref=src, dst_ref=dst, send_sem=send, recv_sem=recv, device_id=(b, hh), device_id_type=MESH
        )

    def to_height(src, dst, send, recv, h):
        return pltpu.make_async_remote_copy(
            src_ref=src, dst_ref=dst, send_sem=send, recv_sem=recv, device_id=(me, h), device_id_type=MESH
        )

    def weight_copy(i, k):
        slot = r.g[i].at[me]
        return to_batch(slot, slot, r.s_wsend.at[i, k], r.s_wrecv.at[i, me], next_batch(k))

    def weight_arrival(i, k):
        b = next_batch(k)
        slot = r.g[i].at[b]
        return to_batch(slot, slot, r.s_wsend.at[i, k], r.s_wrecv.at[i, b], b)

    local[0].wait()
    local[1].wait()
    r.g[0][me] = r.v_in[...].astype(bf16)

    edge_rows = iota((2 * HX, T), 0)
    edge_cols = iota((2 * HX, T), 1)
    edges = (edge_cols == (edge_rows % HX) * R + (edge_rows // HX) * (R - 1)).astype(bf16)
    for n in range(IMG):
        outer = nn(edges, r.v_act[n]).astype(bf16)
        r.hs[0, n] = outer[:HX]
        r.hs[1, n] = outer[HX:]
    above, below = next_height(HG - 1), next_height(1)
    halo_up = to_height(r.hs.at[0], r.hr.at[1], r.s_hsend.at[0], r.s_hrecv.at[0], above)
    halo_down = to_height(r.hs.at[1], r.hr.at[0], r.s_hsend.at[1], r.s_hrecv.at[1], below)

    pl.semaphore_wait(barrier, B - 1 + HG - 1)
    loop(1, B, lambda k: weight_copy(0, k).start())
    halo_up.start()
    halo_down.start()
    for k in (2, 3, 4):
        local[k].wait()
    mine = r.g[1].at[me]
    mine[:, :HID] = r.v_exp[...].astype(bf16)
    for i in range(4):
        mine[:, HID + D * i : HID + D * (i + 1)] = r.v_red[rows * i : rows * (i + 1)].astype(bf16)
    mine[:, HID + 4 * D :] = jnp.concatenate(
        [r.v_out[...], jnp.zeros((rows, PE - HID - 5 * D), f32)], axis=1
    ).astype(bf16)
    loop(1, B, lambda k: weight_copy(1, k).start())

    for k in range(5, 11):
        local[k].wait()
    poolq, poolkv, table = r.poolq, r.poolkv, r.table
    poolq[...] = r.v_pool[:, 0, :]
    poolkv[:, :D] = r.v_pool[:, 1, :]
    poolkv[:, D:] = r.v_pool[:, 2, :]
    r.tablef[...] = jnp.zeros_like(r.tablef)
    relh_rows, relw_rows = r.v_relh.shape[0], r.v_relw.shape[0]
    for hd in range(2):
        r.tablef[128 * hd : 128 * hd + relh_rows, HD * hd : HD * (hd + 1)] = r.v_relh[...]
        r.tablef[128 * hd + 64 : 128 * hd + 64 + relw_rows, HD * hd : HD * (hd + 1)] = r.v_relw[...]
    table[...] = r.tablef[...].astype(bf16)
    shift_one = r.v_biases[0:1, 0:D]
    shift_two = r.v_biases[0:1, D : 2 * D]
    bias_q = r.v_biases[0:1, 2 * D : 3 * D]
    bias_kv = r.v_biases[0:1, 3 * D : 5 * D]
    bias_out = r.v_biases[0:1, 5 * D : 6 * D]
    bias_exp = r.v_biases[0:1, 6 * D : 6 * D + HID]
    bias_red = r.v_biases[0:1, 6 * D + HID : 7 * D + HID]
    gain_one = r.v_gains[0:1, :]
    gain_two = r.v_gains[1:2, :]
    acc, paccq, pacckv = r.acc, r.paccq, r.pacckv
    acc[...] = jnp.zeros_like(acc)
    paccq[...] = jnp.zeros_like(paccq)
    pacckv[...] = jnp.zeros_like(pacckv)
    kvx, qx, dqx = r.kvx, r.qx, r.dqx

    cell = iota((T, 1), 0)
    cell_y, cell_x = hh * R + cell % R, cell // R
    halo_at = iota((2 * IMG * HX, 1), 0)

    def cell_mask(n):
        return ((cell_y < r.extent[0, n]) & (cell_x < r.extent[1, n])).astype(f32)

    def first_norm(n):
        hat, inverse = normalise(r.v_act[n].astype(f32))
        r.ne[n] = (hat * gain_one + shift_one).astype(bf16)
        r.hat_one[n] = hat
        r.inv_one[n] = inverse
        kvx[n, 0:R, :] = jnp.zeros((R, 2 * D), f32)
        kvx[n, T + R :, :] = jnp.zeros((R, 2 * D), f32)
        for x in (qx, dqx):
            x[n, 0:R, :] = jnp.zeros((R, D), f32)
            x[n, T + R :, :] = jnp.zeros((R, D), f32)

    loop(0, IMG, first_norm)

    spread_rows = iota((T, 2 * HX), 0)
    spread_cols = iota((T, 2 * HX), 1)
    spread = (
        (spread_rows // R == spread_cols % HX) & (spread_rows % R == (spread_cols // HX) * (R - 1))
    ).astype(bf16)
    r.spread[...] = jnp.concatenate([spread, spread], axis=1)
    pick_rows = iota((KL * KCP, T // 2), 0)
    pick_cols = iota((KL * KCP, T // 2), 1)
    pick = (
        (pick_rows % KCP == pick_cols // R) & (pick_cols % R == 2 * (pick_rows // KCP))
    ).astype(bf16)
    r.pick[...] = jnp.concatenate([pick, pick], axis=1)
    back_rows = iota((3 * T // 2, KROWS), 0)
    back_cols = iota((3 * T // 2, KROWS), 1)
    back_tap, back_cell = back_rows // (T // 2), back_rows % (T // 2)
    unpick = (
        (back_cols % KCP == back_cell // R)
        & (back_cell % R == 2 * (back_cols // KCP) + back_tap - 1)
    ).astype(bf16)
    r.unpick[...] = jnp.concatenate([unpick, unpick], axis=1)
    key_rows = iota((KEYS, 64), 0)
    key_lane = iota((KEYS, 64), 1) % 32
    r.hot[...] = (
        (key_lane == key_rows // KCP) | (key_lane == KR + key_rows % KCP)
    ).astype(bf16)
    halo_up.wait_recv()
    halo_down.wait_recv()
    hat, _ = normalise(r.hr[...].reshape(2 * IMG * HX, D).astype(f32))
    r.nh[...] = (hat * gain_one + shift_one).astype(bf16)

    halo_y = jnp.where(halo_at < IMG * HX, hh * R - 1, hh * R + R)
    halo_image = halo_at // HX % IMG
    halo_ok = jnp.zeros((2 * IMG * HX, 1), jnp.bool_)
    for n in range(IMG):
        halo_ok = halo_ok | (
            (halo_image == n)
            & (halo_y >= 0)
            & (halo_y < r.extent[0, n])
            & (halo_at % HX < r.extent[1, n])
        )
    halo_ok = halo_ok.astype(f32)

    loop(1, B, lambda k: weight_arrival(0, k).wait_recv())
    wq, wkv, wout, wexp, wred = r.wq, r.wkv, r.wout, r.wexp, r.wred
    for b in range(B):
        shard = r.g[0][b].astype(f32)
        r.f_q[rows * b : rows * (b + 1), :] = shard[:, :D]
        r.f_kv[rows * b : rows * (b + 1), :] = shard[:, D:]
    wq[...] = r.f_q[...].astype(bf16)
    wkv[...] = r.f_kv[...].astype(bf16)

    kvg = r.kvg

    def kv_copy(n, k, source, target):
        slot = kvg.at[source, n]
        return to_height(slot, slot, r.s_ksend.at[n, k - 1], r.s_krecv.at[n, k - 1], target)

    half = IMG * HX
    r.halo_kv[...] = (nn(r.nh[:half], wkv[...]) + bias_kv) * halo_ok[:half]

    def columns(x, b):
        pairs = x.reshape(TX // (2 * R), 2 * R, x.shape[1])
        side = pairs[b // 2 : b // 2 + KC, R * (b % 2) : R * (b % 2) + R]
        return side.reshape(T // 2, x.shape[1])

    def keys_values(n):
        kvx[n, R : R + T, :] = (nn(r.ne[n], wkv[...]) + bias_kv) * cell_mask(n)
        field = kvx[n]
        sides = [columns(field, b) for b in range(3)]
        sums = [sum(poolkv[3 * a + b : 3 * a + b + 1, :] * sides[b] for b in range(3)) for a in range(3)]
        pooled = rolled(sums[0], 1) * (iota((T // 2, 1), 0) % R > 0).astype(f32) + sums[1] + rolled(sums[2], -1)
        edge = r.halo_kv[pl.ds(pl.multiple_of(n * HX, HX), HX), :]
        edge = (
            poolkv[0:1, :] * rolled(edge, 1) + poolkv[1:2, :] * edge + poolkv[2:3, :] * rolled(edge, -1)
        )
        edge_pick = (iota((KCP, HX), 1) == 2 * iota((KCP, HX), 0)).astype(bf16)
        edge = nn(jnp.concatenate([edge_pick, edge_pick], axis=1), halves(edge, 0))
        whole = nn(r.pick[...], halves(pooled, 0))
        kvg[hh, n] = jnp.concatenate([whole[:KCP] + edge, whole[KCP:]], axis=0).astype(bf16)
        for k in range(1, HG):
            kv_copy(n, k, hh, next_height(k)).start()

    loop(0, IMG, keys_values)

    qp, qa = r.qp, r.qa
    r.halo_q[...] = (nn(r.nh[...], wq[...]) + bias_q) * halo_ok
    lane = iota((T, 128), 1)
    y_at = hh * R + iota((T, 128), 0) % R
    x_at = iota((T, 128), 0) // R
    aux = lane % 32
    spot = jnp.where(aux < KR, y_at - 2 * aux + 2 * (KR - 1), 64 + x_at - 2 * (aux - KR) + 2 * (KC - 1))
    inner_top = (cell % R > 0).astype(f32)
    inner_low = (cell % R < R - 1).astype(f32)

    def beside(x):
        return [rolled(x, 1), x, rolled(x, -1)]

    def queries(n):
        qx[n, R : R + T, :] = (nn(r.ne[n], wq[...]) + bias_q) * cell_mask(n)
        field = qx[n]
        sums = [
            sum(poolq[3 * a + b : 3 * a + b + 1, :] * field[R * b : R * b + T] for b in range(3))
            for a in range(3)
        ]
        top = beside(r.halo_q[pl.ds(pl.multiple_of(n * HX, HX), HX), :])
        low = beside(r.halo_q[pl.ds(pl.multiple_of((IMG + n) * HX, HX), HX), :])
        top = sum(poolq[b : b + 1, :] * top[b] for b in range(3))
        low = sum(poolq[6 + b : 7 + b, :] * low[b] for b in range(3))
        edge = nn(r.spread[...], halves(jnp.concatenate([top, low], axis=0), 0))
        pooled = rolled(sums[0], 1) * inner_top + sums[1] + rolled(sums[2], -1) * inner_low + edge
        qp[n] = pooled
        query = pooled.astype(bf16)
        r.qh[n] = query
        along = nt(query, table[...])
        left, right = pooled[:, :128], pooled[:, 128:]
        right = jnp.concatenate([right, right], axis=1)
        for hd in range(2):
            near = along[:, 128 * hd : 128 * (hd + 1)]
            near = jnp.take_along_axis(near, spot, axis=1, mode="promise_in_bounds") * (HD**0.5)
            rest = near - near.astype(bf16).astype(f32)
            near = jnp.where(lane < 96, near, rest)
            if hd == 0:
                qa[n, hd, :, :128] = jnp.where(lane < HD, left, 0.0).astype(bf16)
                qa[n, hd, :, 128:] = jnp.where(lane < 64, 0.0, near).astype(bf16)
            else:
                qa[n, hd, :, :128] = jnp.where(lane < HD, 0.0, left).astype(bf16)
                qa[n, hd, :, 128:] = jnp.where(lane < 64, right, near).astype(bf16)

    loop(0, IMG, queries)

    key_at = iota((KEYS, 1), 0)
    probs, mxh = r.probs, r.mxh

    def attention(n):
        for k in range(1, HG):
            kv_copy(n, k, next_height(HG - k), hh).wait_recv()
        both = jnp.concatenate([kvg[s, n] for s in range(HG)], axis=0)
        r.ka[n, :, :D] = both[:, :D]
        r.ka[n, :, D:] = r.hot[...]
        r.va[n] = both[:, D:]
        valid = (2 * (key_at // KCP) < r.extent[0, n]) & (2 * (key_at % KCP) < r.extent[1, n])
        value = r.va[n].T
        mixed = []
        for hd in range(2):
            scores = nt(r.ka[n], qa[n, hd]) * SCALE
            scores = jnp.where(valid, scores, masked_value)
            raised = jnp.exp(scores - jnp.max(scores, axis=0, keepdims=True))
            prob = raised * (1.0 / jnp.sum(raised, axis=0, keepdims=True))
            probs[n, hd] = prob
            mixed.append(nn(value[HD * hd : HD * (hd + 1)], prob.astype(bf16)))
        mxh[n] = (jnp.concatenate(mixed, axis=0).T + qp[n]).astype(bf16)

    loop(0, IMG, attention)

    loop(1, B, lambda k: weight_arrival(1, k).wait_recv())
    for b in range(B):
        shard = r.g[1][b].astype(f32)
        r.f_exp[rows * b : rows * (b + 1), :] = shard[:, :HID]
        for i in range(4):
            at = 4 * rows * b + rows * i
            r.f_red[at : at + rows, :] = shard[:, HID + D * i : HID + D * (i + 1)]
        r.f_out[rows * b : rows * (b + 1), :] = shard[:, HID + 4 * D : HID + 5 * D]
    wout[...] = r.f_out[...].astype(bf16)
    wexp[...] = r.f_exp[...].astype(bf16)
    wred[...] = r.f_red[...].astype(bf16)

    def feed_forward(n):
        mask = cell_mask(n)
        middle = r.v_act[n].astype(f32) + nn(mxh[n], wout[...]) + bias_out
        hat, inverse = normalise(middle)
        second = (hat * gain_two + shift_two).astype(bf16)
        r.sh[n] = second
        expanded = nn(second, wexp[...]) + bias_exp
        half_erf = 0.5 + 0.5 * lax.erf(expanded * (0.5**0.5))
        activated = (expanded * half_erf).astype(bf16)
        slope = half_erf + expanded * jnp.exp(expanded * expanded * -0.5) * 0.3989422804014327
        r.ac[n] = activated
        r.v_res[n] = (mask * (middle + nn(activated, wred[...]) + bias_red)).astype(bf16)
        upstream = r.v_cot[n].astype(f32) * mask
        up_half = upstream.astype(bf16)
        r.uh[n] = up_half
        expanded_grad = (nt(up_half, wred[...]) * slope).astype(bf16)
        r.eg[n] = expanded_grad
        second_grad = nt(expanded_grad, wexp[...])
        acc[0:1, 2 * D : 3 * D] += jnp.sum(second_grad * hat, axis=0, keepdims=True)
        acc[0:1, 3 * D : 4 * D] += jnp.sum(second_grad, axis=0, keepdims=True)
        middle_grad = upstream + normalise_back(second_grad, gain_two, hat, inverse)
        r.mgd[n] = middle_grad
        attn_grad = middle_grad.astype(bf16)
        r.ag[n] = attn_grad
        r.mg[n] = nt(attn_grad, wout[...]).astype(bf16)

    loop(0, IMG, feed_forward)
    result_out = pltpu.make_async_copy(r.v_res, r.o_res, r.s_out.at[0])
    result_out.start()

    ones = jnp.ones((16, IMG * T), bf16)

    def flat(ref):
        return ref[...].reshape(IMG * T, ref.shape[-1])

    r.f_exp[...] = tn(flat(r.sh), flat(r.eg))
    acc[2:3, :] = nn(ones, flat(r.eg))[0:1]
    r.f_red[...] = tn(flat(r.uh), flat(r.ac)).T
    acc[1:2, D : 2 * D] = nn(ones, flat(r.uh))[0:1]
    r.f_out[...] = tn(flat(mxh), flat(r.ag))
    acc[1:2, 0:D] = nn(ones, flat(r.ag))[0:1]
    for b in range(B):
        r.d[1][b, :, :HID] = r.f_exp[rows * b : rows * (b + 1), :].astype(bf16)
        for i in range(4):
            at = 4 * rows * b + rows * i
            r.d[1][b, :, HID + D * i : HID + D * (i + 1)] = r.f_red[at : at + rows, :].astype(bf16)
        r.d[1][b, :, HID + 4 * D :] = jnp.concatenate(
            [r.f_out[rows * b : rows * (b + 1), :], jnp.zeros((rows, PE - HID - 5 * D), f32)], axis=1
        ).astype(bf16)

    def one_copy(i, k, target):
        return to_height(
            r.d[i].at[pl.ds(target * QB, QB)],
            r.p[i].at[k - 1],
            r.s_onesend.at[i, k - 1],
            r.s_onerecv.at[i, k - 1],
            target,
        )

    for k in range(1, HG):
        one_copy(1, k, next_height(k)).start()

    dkv = r.dkv
    y_lane = jnp.where(lane < 64, y_at + 2 * (KR - 1) - lane, x_at + 2 * (KC - 1) - (lane - 64))
    back_at = y_lane // 2
    back_ok = (y_lane >= 0) & (y_lane % 2 == 0) & (back_at < jnp.where(lane < 64, KR, KC))
    back_spot = jnp.where(back_ok, back_at + jnp.where(lane < 64, 64, 64 + KR), 0)
    back_ok = back_ok.astype(f32)

    def dkv_copy(n, k, target):
        return to_height(
            dkv.at[n, pl.ds(pl.multiple_of(target * (KL * KCP), KL * KCP), KROWS), :],
            r.dkvr.at[k - 1, n],
            r.s_dsend.at[n, k - 1],
            r.s_drecv.at[n, k - 1],
            target,
        )

    def attention_back(n):
        value = r.va[n]
        keys = r.ka[n].T
        mixed_grad = r.mg[n].astype(f32)
        query = r.qh[n].astype(f32)
        head = iota((T, D), 1) < HD
        probs_half, grads_half, dq, along = [], [], [], []
        mixed_heads = [jnp.where(head, mixed_grad, 0.0), jnp.where(head, 0.0, mixed_grad)]
        mixed_heads = [x.astype(bf16) for x in mixed_heads]
        query_heads = [jnp.where(head, query, 0.0), jnp.where(head, 0.0, query)]
        query_heads = [x.astype(bf16) for x in query_heads]
        key_grad, value_grad = 0.0, 0.0
        for hd in range(2):
            prob = probs[n, hd]
            prob_grad = nt(value, mixed_heads[hd])
            inner = jnp.sum(prob * prob_grad, axis=0, keepdims=True)
            score_grad = (prob * (prob_grad - inner)).astype(bf16)
            value_grad = value_grad + nn(prob.astype(bf16), mixed_heads[hd])
            key_grad = key_grad + nn(score_grad, query_heads[hd])
            back = nn(jnp.concatenate([keys[HD * hd : HD * (hd + 1)], keys[D : D + 32]], axis=0), score_grad)
            dq.append(back[:HD])
            along.append(back[HD:])
        dkv[n, 0:KEYS, :D] = (key_grad * SCALE).astype(bf16)
        dkv[n, 0:KEYS, D:] = value_grad.astype(bf16)
        dkv[n, KEYS:, :] = jnp.zeros((dkv.shape[1] - KEYS, 2 * D), bf16)
        for k in range(1, HG):
            dkv_copy(n, k, next_height(k)).start()
        back = jnp.concatenate(dq + along, axis=0).T
        right = back[:, 128:]
        apart = []
        for hd in range(2):
            apart.append(
                jnp.take_along_axis(right, back_spot + 32 * hd, axis=1, mode="promise_in_bounds") * back_ok
            )
        apart = halves(jnp.concatenate(apart, axis=1), 1)
        r.dr[n] = apart
        from_tables = nn(apart, jnp.concatenate([table[...], table[...]], axis=0))
        dqx[n, R : R + T, :] = back[:, :D] * SCALE + from_tables + mixed_grad
        outer = nn(edges, dqx[n, R : R + T, :].astype(bf16)).astype(bf16)
        r.dqs[0, n] = outer[:HX]
        r.dqs[1, n] = outer[HX:]

    loop(0, IMG, attention_back)
    back_up = to_height(r.dqs.at[0], r.dqr.at[1], r.s_qsend.at[0], r.s_qrecv.at[0], above)
    back_down = to_height(r.dqs.at[1], r.dqr.at[0], r.s_qsend.at[1], r.s_qrecv.at[1], below)
    back_up.start()
    back_down.start()

    def two_copy(i, j, b):
        return to_batch(r.t[i].at[j], r.u[i].at[me], r.s_twosend.at[i, j], r.s_tworecv.at[i, me], b)

    def two_arrival(i, b):
        return to_batch(r.t[i].at[0], r.u[i].at[b], r.s_twosend.at[i, 0], r.s_tworecv.at[i, b], b)

    def stage_one(i):
        for k in range(1, HG):
            one_copy(i, k, hh).wait_recv()

        def add(j):
            b = hh * QB + j
            total = r.d[i][b].astype(f32)
            for k in range(HG - 1):
                total = total + r.p[i][k, j].astype(f32)
            r.t[i][j] = total.astype(bf16)

            @pl.when(b != me)
            def _():
                two_copy(i, j, b).start()

        loop(0, QB, add)

    stage_one(1)

    both = tn(flat(r.qh), flat(r.dr))
    rel = (
        both[:HD, 0:128] + both[:HD, 256:384] + both[HD:, 128:256] + both[HD:, 384:512]
    )
    rel = jnp.concatenate([rel, jnp.zeros((128 - HD, 128), f32)], axis=0).T
    for q in range(HG):
        r.smallp[q, 24:, :] = rel[32 * q : 32 * (q + 1)]

    has_above = (hh > 0).astype(f32)
    has_below = (hh < HG - 1).astype(f32)
    back_up.wait_recv()
    back_down.wait_recv()

    def queries_back(n):
        edge = jnp.concatenate([r.dqr[0, n].astype(f32) * has_above, r.dqr[1, n].astype(f32) * has_below], axis=0)
        edge = nn(r.spread[:, : 2 * HX], edge.astype(bf16))
        nothing = jnp.zeros((R, D), f32)
        field = dqx[n]
        whole = field[R : R + T]
        later = jnp.concatenate([nothing, rolled(whole, -1) * inner_low + edge * (1.0 - inner_low), nothing], axis=0)
        sooner = jnp.concatenate([nothing, rolled(whole, 1) * inner_top + edge * (1.0 - inner_top), nothing], axis=0)
        own = qx[n, R : R + T, :]
        total = 0.0
        for a, moved in enumerate((later, field, sooner)):
            for b in range(3):
                here = moved[R * (2 - b) : R * (2 - b) + T]
                total = total + poolq[3 * a + b : 3 * a + b + 1, :] * here
                paccq[3 * a + b] += folded(here * own)
        r.pq[n] = (total * cell_mask(n)).astype(bf16)

    loop(0, IMG, queries_back)

    def keys_values_back(n):
        for k in range(1, HG):
            dkv_copy(n, k, hh).wait_recv()
        total = dkv[n, pl.ds(pl.multiple_of(hh * (KL * KCP), KL * KCP), KROWS), :].astype(f32)
        for k in range(HG - 1):
            total = total + r.dkvr[k, n].astype(f32)
        wide = nn(r.unpick[...], halves(total, 0))
        taps = [wide[T // 2 * a : T // 2 * (a + 1)] for a in range(3)]
        field = kvx[n]
        sides = [columns(field, b) for b in range(3)]
        even, odd, late = 0.0, 0.0, 0.0
        for a in range(3):
            even = even + poolkv[3 * a + 1 : 3 * a + 2, :] * taps[a]
            odd = odd + poolkv[3 * a + 2 : 3 * a + 3, :] * taps[a]
            late = late + poolkv[3 * a : 3 * a + 1, :] * taps[a]
            for b in range(3):
                pacckv[3 * a + b] += folded(sides[b] * taps[a])
        odd = odd + jnp.concatenate([late[R:], jnp.zeros((R, 2 * D), f32)], axis=0)
        pairs = [x.reshape(KC, R, 2 * D) for x in (even, odd)]
        result = jnp.concatenate(pairs, axis=1).reshape(T, 2 * D)
        r.pkv[n] = (result * cell_mask(n)).astype(bf16)

    loop(0, IMG, keys_values_back)

    r.f_q[...] = tn(flat(r.ne), flat(r.pq))
    r.f_kv[...] = tn(flat(r.ne), flat(r.pkv))
    for b in range(B):
        at = slice(rows * b, rows * (b + 1))
        r.d[0][b] = jnp.concatenate([r.f_q[at, :], r.f_kv[at, :]], axis=1).astype(bf16)
    for k in range(1, HG):
        one_copy(0, k, next_height(k)).start()

    def projection_back(n):
        grad = nt(r.pq[n], wq[...]) + nt(r.pkv[n], wkv[...])
        hat = r.hat_one[n]
        acc[0:1, 0:D] += jnp.sum(grad * hat, axis=0, keepdims=True)
        acc[0:1, D : 2 * D] += jnp.sum(grad, axis=0, keepdims=True)
        r.v_ig[n] = r.mgd[n] + normalise_back(grad, gain_one, hat, r.inv_one[n])

    loop(0, IMG, projection_back)
    input_out = pltpu.make_async_copy(r.v_ig, r.o_ig, r.s_out.at[1])
    input_out.start()

    small = r.small
    small[...] = jnp.zeros_like(small)
    for t in range(9):
        small[t : t + 1, 0:D] = jnp.sum(paccq[t], axis=0, keepdims=True)
        small[t : t + 1, D : 3 * D] = jnp.sum(pacckv[t], axis=0, keepdims=True)
    small[9:10, 0:D] = nn(ones, flat(r.pq))[0:1]
    small[9:10, D : 3 * D] = nn(ones, flat(r.pkv))[0:1]
    small[10:13, :] = acc[...]
    for q in range(HG):
        for i in range(6):
            r.smallp[q, 4 * i : 4 * (i + 1), :] = small[4 * q : 4 * (q + 1), 128 * i : 128 * (i + 1)]

    def small_one(k, target):
        return to_height(
            r.smallp.at[target], r.smallr.at[k - 1], r.s_smallsend.at[k - 1], r.s_smallrecv.at[k - 1], target
        )

    for k in range(1, HG):
        small_one(k, next_height(k)).start()

    def small_two(k):
        slot = r.smallu.at[me]
        return to_batch(slot, slot, r.s_smalltwo.at[k], r.s_smalltwor.at[me], next_batch(k))

    def small_two_arrival(k):
        b = next_batch(k)
        slot = r.smallu.at[b]
        return to_batch(slot, slot, r.s_smalltwo.at[k], r.s_smalltwor.at[b], b)

    stage_one(0)
    for k in range(1, HG):
        small_one(k, hh).wait_recv()
    total = r.smallp[hh]
    for k in range(HG - 1):
        total = total + r.smallr[k]
    r.smallu[me] = total
    loop(1, B, lambda k: small_two(k).start())

    owned = me // QB == hh
    spans = (slice(PE, PE + PI), slice(0, PE))

    def three_copy(i, k):
        return to_height(
            r.z[i], r.z[i], r.s_threesend.at[i, k - 1], r.s_threerecv.at[i], next_height(k)
        )

    @pl.when(owned)
    def _():
        for i in (1, 0):
            loop(1, B, lambda k, i=i: two_arrival(i, next_batch(k)).wait_recv())
            r.u[i][me] = r.t[i][me - hh * QB]
            total = r.u[i][0].astype(f32)
            for b in range(1, B):
                total = total + r.u[i][b].astype(f32)
            r.z[i][...] = total
            for k in range(1, HG):
                three_copy(i, k).start()

    def small_three(k):
        slot = r.smallz.at[hh]
        return to_height(slot, slot, r.s_smallthree.at[k - 1], r.s_smallthreer.at[k - 1], next_height(k))

    def small_three_arrival(k):
        slot = r.smallz.at[next_height(HG - k)]
        return to_height(slot, slot, r.s_smallthree.at[k - 1], r.s_smallthreer.at[k - 1], next_height(k))

    loop(1, B, lambda k: small_two_arrival(k).wait_recv())
    total = r.smallu[0]
    for b in range(1, B):
        total = total + r.smallu[b]
    r.smallz[hh] = total
    for k in range(1, HG):
        small_three(k).start()

    @pl.when(jnp.logical_not(owned))
    def _():
        for i in range(2):
            three_copy(i, 1).wait_recv()

    for k in range(1, HG):
        small_three_arrival(k).wait_recv()
    outs = [(r.z[0], r.o_z[0]), (r.z[1], r.o_z[1]), (r.smallz, r.o_small)]
    outs = [pltpu.make_async_copy(a, b, r.s_out.at[2 + k]) for k, (a, b) in enumerate(outs)]
    for out in outs:
        out.start()

    for copy in (halo_up, halo_down, back_up, back_down):
        copy.wait_send()
    for i in range(2):
        loop(1, B, lambda k, i=i: weight_copy(i, k).wait_send())
    for k in range(1, HG):
        for n in range(IMG):
            kv_copy(n, k, hh, next_height(k)).wait_send()
            dkv_copy(n, k, next_height(k)).wait_send()
        for i in range(2):
            one_copy(i, k, next_height(k)).wait_send()
        small_one(k, next_height(k)).wait_send()
        small_three(k).wait_send()

    def sent_two(j):
        @pl.when(hh * QB + j != me)
        def _():
            for i in range(2):
                two_copy(i, j, hh * QB + j).wait_send()

    loop(0, QB, sent_two)
    loop(1, B, lambda k: small_two(k).wait_send())

    @pl.when(owned)
    def _():
        for i in range(2):
            for k in range(1, HG):
                three_copy(i, k).wait_send()

    result_out.wait()
    input_out.wait()
    for out in outs:
        out.wait()


def adam_step(weight, first_state, second_state, gradient, step_rate, decay_rate):
    moment = beta_one * first_state + (1.0 - beta_one) * gradient
    square = beta_two * second_state + (1.0 - beta_two) * gradient * gradient
    unbiased = moment * (1.0 / (1.0 - beta_one**STEP))
    scaled = square * (1.0 / (1.0 - beta_two**STEP))
    updated = weight * (1.0 - step_rate * decay_rate) - step_rate * unbiased / (jnp.sqrt(scaled) + adam_eps)
    return (updated, moment, square)


def adam_kernel(tree, *refs):
    r = types.SimpleNamespace(**jax.tree.unflatten(tree, refs))

    def row(ref):
        return ref.at[0] if ref.shape[0] == 1 and len(ref.shape) == 2 else ref

    arrivals = []
    for index, (source, target) in enumerate(zip(r.given, r.v_given)):
        arrivals.append(pltpu.make_async_copy(source, row(target), r.s_in.at[index]))
        arrivals[-1].start()
    rows = r.v_given[0].shape[0]
    small = r.small
    for i in range(4):
        arrivals[i].wait()
    for q in range(HG):
        for i in range(6):
            small[4 * q : 4 * (q + 1), 128 * i : 128 * (i + 1)] = r.v_given[2][q, 4 * i : 4 * (i + 1), :]
    rel = jnp.concatenate([r.v_given[2][q, 24:, :] for q in range(HG)], axis=0)
    for t in range(9):
        for i in range(3):
            r.pgrad[t, i : i + 1, :] = small[t : t + 1, D * i : D * (i + 1)]
    bgrad = r.bgrad
    bgrad[0:1, 0:D] = small[10:11, D : 2 * D]
    bgrad[0:1, D : 2 * D] = small[10:11, 3 * D :]
    bgrad[0:1, 2 * D : 5 * D] = small[9:10, : 3 * D]
    bgrad[0:1, 5 * D : 6 * D] = small[11:12, 0:D]
    bgrad[0:1, 6 * D : 6 * D + HID] = small[12:13, :]
    bgrad[0:1, 6 * D + HID :] = small[11:12, D : 2 * D]
    pack = r.v_given[1]
    given = [r.v_given[3 + 3 * index : 6 + 3 * index] for index in range(9)]
    gradients = [
        lambda: r.v_given[0][...],
        lambda: pack[:, HID + 4 * D : HID + 5 * D],
        lambda: pack[:, :HID],
        lambda: jnp.concatenate([pack[:, HID + D * i : HID + D * (i + 1)] for i in range(4)], axis=0),
        lambda: r.pgrad[...],
        lambda: rel[0 : given[5][0].shape[0], 0:HD],
        lambda: rel[64 : 64 + given[6][0].shape[0], 0:HD],
        lambda: jnp.concatenate([small[10:11, 0:D], small[10:11, 2 * D : 3 * D]], axis=0),
        lambda: bgrad[...],
    ]
    leaving = []

    def leave(index):
        copy = pltpu.make_async_copy(row(r.v_fresh[index]), r.fresh[index], r.s_out.at[index])
        copy.start()
        leaving.append(copy)

    for index in range(9):
        for k in range(3):
            if index or k:
                arrivals[3 + 3 * index + k].wait()
        weight, first, second = [x[...] for x in given[index]]
        fresh = adam_step(
            weight, first, second, gradients[index](), step_rates[index], decay_rates[index]
        )
        if index < 4:
            fresh += (fresh[0].astype(bf16),)
        at = 4 * min(index, 4) + 3 * max(index - 4, 0)
        for k, value in enumerate(fresh):
            r.v_fresh[at + k][...] = value
            leave(at + k)
    for copy in leaving:
        copy.wait()


def shards(activations, cotangent, extent, *params):
    B = lax.axis_size("batch")
    assert lax.axis_size("height") == HG and activations.shape == (IMG, R, C, D)
    params = list(params)
    for k in range(12, 15):
        params[k] = params[k].transpose(1, 0, 2)
    weights = params[0::3]
    rows = weights[0].shape[0]
    QB = B // HG
    assert weights[3].shape[0] == 4 * rows

    def by_column(x):
        return x.transpose(0, 2, 1, 3).reshape(IMG, T, D)

    def like(x):
        return jax.ShapeDtypeStruct(x.shape, x.dtype)

    anywhere = pl.BlockSpec(memory_space=pl.ANY)
    vm, dma = pltpu.VMEM, pltpu.SemaphoreType.DMA

    def call(kernel, operands, results, scratch, specs, **kwargs):
        flat_operands, operand_tree = jax.tree.flatten(operands)
        flat_results, result_tree = jax.tree.flatten(results)
        whole, tree = jax.tree.flatten({**operands, **results, **scratch})
        order = {id(x): k for k, x in enumerate(flat_operands + flat_results + jax.tree.leaves(scratch))}
        places = [order[id(x)] for x in whole]

        def ordered(*refs):
            return kernel(tree, *[refs[k] for k in places])

        out = pl.pallas_call(
            ordered,
            out_shape=flat_results,
            in_specs=[specs.get(id(x), anywhere) for x in flat_operands],
            out_specs=[anywhere] * len(flat_results),
            scratch_shapes=jax.tree.leaves(scratch),
            **kwargs,
        )(*flat_operands)
        return jax.tree.unflatten(result_tree, out)

    operands = dict(
        act=by_column(activations),
        cot=by_column(cotangent),
        extent=extent.T,
        w_in=weights[0],
        w_out=weights[1],
        w_exp=weights[2],
        w_red=weights[3],
        pool=weights[4],
        relh=weights[5],
        relw=weights[6],
        gains=weights[7],
        biases=weights[8],
    )
    results = dict(
        o_res=jax.ShapeDtypeStruct((IMG, T, D), bf16),
        o_ig=jax.ShapeDtypeStruct((IMG, T, D), f32),
        o_z=[jax.ShapeDtypeStruct((rows, PI), f32), jax.ShapeDtypeStruct((rows, PE), f32)],
        o_small=jax.ShapeDtypeStruct((HG, 56, 128), f32),
    )
    lanes = (PI, PE)
    scratch = dict(
        v_act=vm((IMG, T, D), bf16),
        v_cot=vm((IMG, T, D), bf16),
        v_in=vm(weights[0].shape, f32),
        v_out=vm(weights[1].shape, f32),
        v_exp=vm(weights[2].shape, f32),
        v_red=vm(weights[3].shape, f32),
        v_pool=vm(weights[4].shape, f32),
        v_relh=vm(weights[5].shape, f32),
        v_relw=vm(weights[6].shape, f32),
        v_gains=vm(weights[7].shape, f32),
        v_biases=vm((1,) + weights[8].shape, f32),
        g=[vm((B, rows, x), bf16) for x in lanes],
        d=[vm((B, rows, x), bf16) for x in lanes],
        p=[vm((HG - 1, QB, rows, x), bf16) for x in lanes],
        t=[vm((QB, rows, x), bf16) for x in lanes],
        u=[vm((B, rows, x), bf16) for x in lanes],
        z=[vm((rows, x), f32) for x in lanes],
        f_q=vm((D, D), f32),
        f_kv=vm((D, 2 * D), f32),
        f_exp=vm((D, HID), f32),
        f_red=vm((HID, D), f32),
        f_out=vm((D, D), f32),
        wq=vm((D, D), bf16),
        wkv=vm((D, 2 * D), bf16),
        wout=vm((D, D), bf16),
        wexp=vm((D, HID), bf16),
        wred=vm((HID, D), bf16),
        poolq=vm((9, D), f32),
        poolkv=vm((9, 2 * D), f32),
        tablef=vm((256, D), f32),
        table=vm((256, D), bf16),
        hs=vm((2, IMG, HX, D), bf16),
        hr=vm((2, IMG, HX, D), bf16),
        nh=vm((2 * IMG * HX, D), bf16),
        halo_q=vm((2 * IMG * HX, D), f32),
        halo_kv=vm((IMG * HX, 2 * D), f32),
        spread=vm((T, 4 * HX), bf16),
        pick=vm((KL * KCP, T), bf16),
        unpick=vm((3 * T // 2, 2 * KROWS), bf16),
        hot=vm((KEYS, 64), bf16),
        acc=vm((3, HID), f32),
        paccq=vm((9, 8, D), f32),
        pacckv=vm((9, 8, 2 * D), f32),
        ne=vm((IMG, T, D), bf16),
        hat_one=vm((IMG, T, D), f32),
        inv_one=vm((IMG, T, 1), f32),
        kvx=vm((IMG, TX, 2 * D), f32),
        qx=vm((IMG, TX, D), f32),
        dqx=vm((IMG, TX, D), f32),
        kvg=vm((HG, IMG, KL * KCP, 2 * D), bf16),
        ka=vm((IMG, KEYS, 256), bf16),
        va=vm((IMG, KEYS, D), bf16),
        qp=vm((IMG, T, D), f32),
        qh=vm((IMG, T, D), bf16),
        qa=vm((IMG, 2, T, 256), bf16),
        probs=vm((IMG, 2, KEYS, T), f32),
        mxh=vm((IMG, T, D), bf16),
        sh=vm((IMG, T, D), bf16),
        ac=vm((IMG, T, HID), bf16),
        uh=vm((IMG, T, D), bf16),
        eg=vm((IMG, T, HID), bf16),
        mgd=vm((IMG, T, D), f32),
        ag=vm((IMG, T, D), bf16),
        mg=vm((IMG, T, D), bf16),
        v_res=vm((IMG, T, D), bf16),
        v_ig=vm((IMG, T, D), f32),
        dkv=vm((IMG, KEYS + KL * KCP, 2 * D), bf16),
        dkvr=vm((HG - 1, IMG, KROWS, 2 * D), bf16),
        dqs=vm((2, IMG, HX, D), bf16),
        dqr=vm((2, IMG, HX, D), bf16),
        dr=vm((IMG, T, 512), bf16),
        pq=vm((IMG, T, D), bf16),
        pkv=vm((IMG, T, 2 * D), bf16),
        small=vm((16, HID), f32),
        smallp=vm((HG, 56, 128), f32),
        smallr=vm((HG - 1, 56, 128), f32),
        smallu=vm((B, 56, 128), f32),
        smallz=vm((HG, 56, 128), f32),
        s_local=dma((11,)),
        s_out=dma((5,)),
        s_wsend=dma((2, B)),
        s_wrecv=dma((2, B)),
        s_hsend=dma((2,)),
        s_hrecv=dma((2,)),
        s_ksend=dma((IMG, HG - 1)),
        s_krecv=dma((IMG, HG - 1)),
        s_dsend=dma((IMG, HG - 1)),
        s_drecv=dma((IMG, HG - 1)),
        s_qsend=dma((2,)),
        s_qrecv=dma((2,)),
        s_onesend=dma((2, HG - 1)),
        s_onerecv=dma((2, HG - 1)),
        s_smallsend=dma((HG - 1,)),
        s_smallrecv=dma((HG - 1,)),
        s_twosend=dma((2, QB)),
        s_tworecv=dma((2, B)),
        s_smalltwo=dma((B,)),
        s_smalltwor=dma((B,)),
        s_threesend=dma((2, HG - 1)),
        s_threerecv=dma((2,)),
        s_smallthree=dma((HG - 1,)),
        s_smallthreer=dma((HG - 1,)),
    )
    main = call(
        functools.partial(main_kernel, B),
        operands,
        results,
        scratch,
        {id(operands["extent"]): pl.BlockSpec(memory_space=pltpu.SMEM)},
        compiler_params=pltpu.CompilerParams(
            collective_id=0, has_side_effects=True, vmem_limit_bytes=52 * 1024 * 1024
        ),
        name="block",
    )
    given = main["o_z"] + [main["o_small"]] + params
    fresh = []
    for index in range(9):
        fresh += [like(weights[index]) for _ in range(3)]
        if index < 4:
            fresh += [jax.ShapeDtypeStruct(weights[index].shape, bf16)]

    def room(x):
        return vm((1,) + x.shape if len(x.shape) == 1 else x.shape, x.dtype)

    fresh = call(
        adam_kernel,
        dict(given=given),
        dict(fresh=fresh),
        dict(
            v_given=[room(x) for x in given],
            v_fresh=[room(x) for x in fresh],
            small=vm((16, HID), f32),
            pgrad=vm(weights[4].shape, f32),
            bgrad=vm((1,) + weights[8].shape, f32),
            s_in=dma((len(given),)),
            s_out=dma((len(fresh),)),
        ),
        {},
        name="adam",
    )["fresh"]
    for k in range(16, 19):
        fresh[k] = fresh[k].transpose(1, 0, 2)

    def by_row(x):
        return x.reshape(IMG, C, R, D).transpose(0, 2, 1, 3)

    return (by_row(main["o_res"]), by_row(main["o_ig"])) + tuple(fresh)


def solution(mesh):
    grid = P("batch", "height", None, None)
    rows = P("batch", None)
    in_specs = (grid, grid, rows) + (rows,) * 12 + (P(),) * 15
    out_specs = (grid, grid) + (rows,) * 16 + (P(),) * 15
    return jax.shard_map(shards, mesh=mesh, in_specs=in_specs, out_specs=out_specs, check_vma=False)
```

time: 1010 us -> 89.1 us (0.09)
  the two profiles are of different devices: /device:TPU:0 before, /device:TPU:25 now
where the time goes in v1:
time: 89.1 us; the launch traced here: 88.3 us
  Pallas kernels  74.6 us (84%)
  local copies, waits for them, and re-layouts  13 us (15%)
    pallas_call x2, Pallas kernels, call(): pl.pallas_call(ordered, out_shape=flat_results, in_specs=[specs.get(id(x)...  74.6 us
    unnamed x34, local copies, waits for them, and re-layouts  13 us

profile of v1, /device:TPU:25, one launch (start us, length us, event | category | flops | bytes accessed | tf_op | source)
XLA Modules:
  0.0 88.3 jit_solution(7379852905475061291)
XLA Ops:
  0.7 0.0 copy-start.13
  0.7 0.0 copy-start.14
  0.7 0.7 copy-done.13
  1.4 0.0 copy-done.14
  1.4 0.0 copy-start
  1.4 0.9 %copy-done = f32[96,192]{1,0:T(8,128)S(1)} copy-done((f32[96,192]{1,0:T(8,128)S(1)}, f32[96,192]{1,0:T(8,128)}, u32[]{:S(2)}) %copy-start) | copy-done | bytes 73752
  2.3 0.0 copy-start.1
  2.3 1.0 %copy-done.1 = bf16[3,8,28,192]{3,1,2,0:T(8,128)(2,1)S(1)} copy-done((bf16[3,8,28,192]{3,1,2,0:T(8,128)(2,1)S(1)}, bf16[3,8,28,192]{3,1,2,0:T(8,128)(2,1)}, u32[]{:S(2)}) %copy-start.1) | copy-done | bytes 258072
  3.3 0.0 copy-start.2
  3.3 1.0 %copy-done.2 = bf16[3,8,28,192]{3,1,2,0:T(8,128)(2,1)S(1)} copy-done((bf16[3,8,28,192]{3,1,2,0:T(8,128)(2,1)S(1)}, bf16[3,8,28,192]{3,1,2,0:T(8,128)(2,1)}, u32[]{:S(2)}) %copy-start.2) | copy-done | bytes 258072
  4.2 0.0 copy-start.3
  4.2 0.9 copy-done.3
  5.1 0.0 copy-start.4
  5.1 0.8 copy-done.4
  5.9 0.0 copy-start.6
  5.9 0.8 copy-done.6
  6.7 0.0 copy-start.7
  6.7 0.8 copy-done.7
  7.5 0.0 copy-start.9
  7.5 0.7 copy-done.9
  8.2 0.0 copy-start.10
  8.2 0.7 copy-done.10
  9.0 0.0 copy-start.12
  9.0 0.7 copy-done.12
  9.7 71.8 %block.1 = (f32[3,224,192]{2,1,0:T(8,128)}, bf16[3,224,192]{2,1,0:T(8,128)(2,1)S(1)}, f32[4,56,128]{2,1,0:T(8,128)S(1)}, f32[24,576]{1,0:T(8,128)S(1)}, f32[24,1792]{1,0:T(8,128)S(1)}) custom-call(bf16[3,224,192]{2,1,0:T(8,128)(2,1)S(1)} %bitcast.19, f32[2112]{0:T(1024)S(1)} %copy-done.12, bf16[3,224,192]{2,1,0:T(8,128)(2,1)S(1)} %bitcast.20, ...), custom_call_target="tpu_custom_call" | custom-call | tf_op jit(solution)/shard_map/block/pallas_call | solution.py:840
  81.5 0.0 copy-start.5
  81.5 0.7 copy-done.5
  82.2 0.0 copy-start.8
  82.2 0.6 copy-done.8
  82.8 0.0 copy-start.11
  82.8 0.6 copy-done.11
  83.5 2.8 %adam.1 = (f32[24,576]{1,0:T(8,128)}, f32[24,576]{1,0:T(8,128)}, f32[24,576]{1,0:T(8,128)}, bf16[24,576]{1,0:T(8,128)(2,1)}, f32[24,192]{1,0:T(8,128)}, /*index=...) custom-call(f32[24,576]{1,0:T(8,128)} %copy-done.11, ...), custom_call_target="tpu_custom_call" | custom-call | tf_op jit(solution)/shard_map/adam/pallas_call | solution.py:840
  86.3 0.0 copy-start.15
  86.3 0.7 copy.65
  87.0 0.5 copy-done.15
  87.5 0.8 copy.66
Async XLA Ops:
  0.7 0.7 copy-start.13
  0.7 0.7 copy-start.14
  1.4 0.9 %copy-start = (f32[96,192]{1,0:T(8,128)S(1)}, f32[96,192]{1,0:T(8,128)}, u32[]{:S(2)}) copy-start(f32[96,192]{1,0:T(8,128)} %refs_12_.1) | copy-start | bytes 221188
  2.3 1.0 %copy-start.1 = (bf16[3,8,28,192]{3,1,2,0:T(8,128)(2,1)S(1)}, bf16[3,8,28,192]{3,1,2,0:T(8,128)(2,1)}, u32[]{:S(2)}) copy-start(bf16[3,8,28,192]{3,1,2,0:T(8,128)(2,1)} %param.30) | copy-start | bytes 774148
  3.3 1.0 %copy-start.2 = (bf16[3,8,28,192]{3,1,2,0:T(8,128)(2,1)S(1)}, bf16[3,8,28,192]{3,1,2,0:T(8,128)(2,1)}, u32[]{:S(2)}) copy-start(bf16[3,8,28,192]{3,1,2,0:T(8,128)(2,1)} %param.31) | copy-start | bytes 774148
  4.2 0.9 %copy-start.3 = (f32[24,768]{1,0:T(8,128)S(1)}, f32[24,768]{1,0:T(8,128)}, u32[]{:S(2)}) copy-start(f32[24,768]{1,0:T(8,128)} %refs_9_.3) | copy-start | bytes 221188
  5.1 0.8 copy-start.4
  5.9 0.8 copy-start.6
  6.7 0.8 copy-start.7
  7.5 0.7 copy-start.9
  8.2 0.7 copy-start.10
  9.0 0.7 copy-start.12
  81.5 0.7 copy-start.5
  82.2 0.6 copy-start.8
  82.8 0.6 copy-start.11
  86.3 1.2 %copy-start.15 = (f32[3,224,192]{2,1,0:T(8,128)S(1)}, f32[3,224,192]{2,1,0:T(8,128)}, u32[]{:S(2)}) copy-start(f32[3,224,192]{2,1,0:T(8,128)} %get-tuple-element.70) | copy-start | bytes 1548292

commit v2 on v1

--- a/solution.py
+++ b/solution.py
@@ -31,8 +31,8 @@
 SCALE = HD ** (-0.5)
 KROWS = (KL + 1) * KCP
 HX = 32
-PE = HID + 4 * D + 2 * 128
-PI = 3 * D
+PH = HID + 128
+PE = 2 * PH
 
 
 def nn(a, b):
@@ -82,8 +82,13 @@
     r = types.SimpleNamespace(**jax.tree.unflatten(tree, refs))
     me = lax.axis_index("batch")
     hh = lax.axis_index("height")
-    QB = B // HG
+    HB = B // 2
     rows = r.w_in.shape[0]
+    side = lax.rem(hh, 2)
+    pair = lax.div(hh, 2)
+    twin = hh + 1 - 2 * side
+    across = lax.rem(hh + 2, HG)
+    corner = lax.rem(twin + 2, HG)
 
     def loop(first, last, body):
         def step(i, carry):
@@ -134,18 +139,31 @@
             src_ref=src, dst_ref=dst, send_sem=send, recv_sem=recv, device_id=(me, h), device_id_type=MESH
         )
 
-    def weight_copy(i, k):
-        slot = r.g[i].at[me]
-        return to_batch(slot, slot, r.s_wsend.at[i, k], r.s_wrecv.at[i, me], next_batch(k))
-
-    def weight_arrival(i, k):
+    def in_copy(k):
+        slot = r.gin.at[me]
+        return to_batch(slot, slot, r.s_wsend.at[0, k], r.s_wrecv.at[0, me], next_batch(k))
+
+    def in_arrival(k):
         b = next_batch(k)
-        slot = r.g[i].at[b]
-        return to_batch(slot, slot, r.s_wsend.at[i, k], r.s_wrecv.at[i, b], b)
+        slot = r.gin.at[b]
+        return to_batch(slot, slot, r.s_wsend.at[0, k], r.s_wrecv.at[0, b], b)
+
+    def rest_copy(k):
+        slot = r.grest.at[side, me]
+        return to_batch(slot, slot, r.s_wsend.at[1, k], r.s_wrecv.at[1, me], next_batch(k))
+
+    def rest_arrival(k):
+        b = next_batch(k)
+        slot = r.grest.at[side, b]
+        return to_batch(slot, slot, r.s_wsend.at[1, k], r.s_wrecv.at[1, b], b)
+
+    def rest_handed(half, target):
+        slot = r.grest.at[half]
+        return to_height(slot, slot, r.s_wsend.at[0, 0], r.s_wrecv.at[2, 0], target)
 
     local[0].wait()
     local[1].wait()
-    r.g[0][me] = r.v_in[...].astype(bf16)
+    r.gin[me] = r.v_in[...].astype(bf16)
 
     edge_rows = iota((2 * HX, T), 0)
     edge_cols = iota((2 * HX, T), 1)
@@ -159,19 +177,17 @@
     halo_down = to_height(r.hs.at[1], r.hr.at[0], r.s_hsend.at[1], r.s_hrecv.at[1], below)
 
     pl.semaphore_wait(barrier, B - 1 + HG - 1)
-    loop(1, B, lambda k: weight_copy(0, k).start())
+    loop(1, B, lambda k: in_copy(k).start())
     halo_up.start()
     halo_down.start()
     for k in (2, 3, 4):
         local[k].wait()
-    mine = r.g[1].at[me]
-    mine[:, :HID] = r.v_exp[...].astype(bf16)
-    for i in range(4):
-        mine[:, HID + D * i : HID + D * (i + 1)] = r.v_red[rows * i : rows * (i + 1)].astype(bf16)
-    mine[:, HID + 4 * D :] = jnp.concatenate(
-        [r.v_out[...], jnp.zeros((rows, PE - HID - 5 * D), f32)], axis=1
-    ).astype(bf16)
-    loop(1, B, lambda k: weight_copy(1, k).start())
+    spare = jnp.zeros((rows, PE - HID - 5 * D), f32)
+    left = jnp.concatenate([r.v_exp[...], r.v_out[:, :128]], axis=1)
+    blocks = [r.v_red[rows * i : rows * (i + 1)] for i in range(4)]
+    right = jnp.concatenate(blocks + [r.v_out[:, 128:], spare], axis=1)
+    r.grest[side, me] = jnp.where(side == 0, left, right).astype(bf16)
+    loop(1, B, lambda k: rest_copy(k).start())
 
     for k in range(5, 11):
         local[k].wait()
@@ -262,10 +278,10 @@
         )
     halo_ok = halo_ok.astype(f32)
 
-    loop(1, B, lambda k: weight_arrival(0, k).wait_recv())
+    loop(1, B, lambda k: in_arrival(k).wait_recv())
     wq, wkv, wout, wexp, wred = r.wq, r.wkv, r.wout, r.wexp, r.wred
     for b in range(B):
-        shard = r.g[0][b].astype(f32)
+        shard = r.gin[b].astype(f32)
         r.f_q[rows * b : rows * (b + 1), :] = shard[:, :D]
         r.f_kv[rows * b : rows * (b + 1), :] = shard[:, D:]
     wq[...] = r.f_q[...].astype(bf16)
@@ -275,7 +291,7 @@
 
     def kv_copy(n, k, source, target):
         slot = kvg.at[source, n]
-        return to_height(slot, slot, r.s_ksend.at[n, k - 1], r.s_krecv.at[n, k - 1], target)
+        return to_height(slot, slot, r.s_ksend.at[n, k], r.s_krecv.at[n, k], target)
 
     half = IMG * HX
     r.halo_kv[...] = (nn(r.nh[:half], wkv[...]) + bias_kv) * halo_ok[:half]
@@ -299,8 +315,8 @@
         edge = nn(jnp.concatenate([edge_pick, edge_pick], axis=1), halves(edge, 0))
         whole = nn(r.pick[...], halves(pooled, 0))
         kvg[hh, n] = jnp.concatenate([whole[:KCP] + edge, whole[KCP:]], axis=0).astype(bf16)
-        for k in range(1, HG):
-            kv_copy(n, k, hh, next_height(k)).start()
+        kv_copy(n, 1, hh, across).start()
+        kv_copy(n, 0, hh, twin).start()
 
     loop(0, IMG, keys_values)
 
@@ -350,12 +366,20 @@
 
     loop(0, IMG, queries)
 
+    def kv_on(n):
+        kv_copy(n, 1, across, hh).wait_recv()
+        kv_copy(n, 2, across, twin).start()
+
+    loop(0, IMG, kv_on)
+    loop(1, B, lambda k: rest_arrival(k).wait_recv())
+    rest_handed(side, twin).start()
+
     key_at = iota((KEYS, 1), 0)
     probs, mxh = r.probs, r.mxh
 
     def attention(n):
-        for k in range(1, HG):
-            kv_copy(n, k, next_height(HG - k), hh).wait_recv()
+        kv_copy(n, 0, twin, hh).wait_recv()
+        kv_copy(n, 2, corner, hh).wait_recv()
         both = jnp.concatenate([kvg[s, n] for s in range(HG)], axis=0)
         r.ka[n, :, :D] = both[:, :D]
         r.ka[n, :, D:] = r.hot[...]
@@ -374,14 +398,15 @@
 
     loop(0, IMG, attention)
 
-    loop(1, B, lambda k: weight_arrival(1, k).wait_recv())
+    rest_handed(1 - side, hh).wait_recv()
     for b in range(B):
-        shard = r.g[1][b].astype(f32)
-        r.f_exp[rows * b : rows * (b + 1), :] = shard[:, :HID]
+        one, two = r.grest[0, b].astype(f32), r.grest[1, b].astype(f32)
+        r.f_exp[rows * b : rows * (b + 1), :] = one[:, :HID]
         for i in range(4):
             at = 4 * rows * b + rows * i
-            r.f_red[at : at + rows, :] = shard[:, HID + D * i : HID + D * (i + 1)]
-        r.f_out[rows * b : rows * (b + 1), :] = shard[:, HID + 4 * D : HID + 5 * D]
+            r.f_red[at : at + rows, :] = two[:, D * i : D * (i + 1)]
+        r.f_out[rows * b : rows * (b + 1), :128] = one[:, HID:]
+        r.f_out[rows * b : rows * (b + 1), 128:] = two[:, 4 * D : 5 * D - 128]
     wout[...] = r.f_out[...].astype(bf16)
     wexp[...] = r.f_exp[...].astype(bf16)
     wred[...] = r.f_red[...].astype(bf16)
@@ -427,26 +452,105 @@
     acc[1:2, D : 2 * D] = nn(ones, flat(r.uh))[0:1]
     r.f_out[...] = tn(flat(mxh), flat(r.ag))
     acc[1:2, 0:D] = nn(ones, flat(r.ag))[0:1]
+    spare = jnp.zeros((rows, PE - HID - 5 * D), f32)
     for b in range(B):
         r.d[1][b, :, :HID] = r.f_exp[rows * b : rows * (b + 1), :].astype(bf16)
-        for i in range(4):
-            at = 4 * rows * b + rows * i
-            r.d[1][b, :, HID + D * i : HID + D * (i + 1)] = r.f_red[at : at + rows, :].astype(bf16)
-        r.d[1][b, :, HID + 4 * D :] = jnp.concatenate(
-            [r.f_out[rows * b : rows * (b + 1), :], jnp.zeros((rows, PE - HID - 5 * D), f32)], axis=1
-        ).astype(bf16)
-
-    def one_copy(i, k, target):
+        out_rows = r.f_out[rows * b : rows * (b + 1), :]
+        r.d[1][b, :, HID:PH] = out_rows[:, :128].astype(bf16)
+        blocks = [r.f_red[rows * (4 * b + i) : rows * (4 * b + i + 1), :] for i in range(4)]
+        r.d[1][b, :, PH:] = jnp.concatenate(blocks + [out_rows[:, 128:], spare], axis=1).astype(bf16)
+
+    def one_copy(i, half, target):
         return to_height(
-            r.d[i].at[pl.ds(target * QB, QB)],
-            r.p[i].at[k - 1],
-            r.s_onesend.at[i, k - 1],
-            r.s_onerecv.at[i, k - 1],
-            target,
+            r.d[i].at[pl.ds(half * HB, HB)], r.p[i], r.s_onesend.at[i], r.s_onerecv.at[i], target
         )
 
-    for k in range(1, HG):
-        one_copy(1, k, next_height(k)).start()
+    def two_copy(i, j, b):
+        return to_batch(r.t[i].at[j], r.u[i].at[me], r.s_twosend.at[i, j], r.s_tworecv.at[i, me], b)
+
+    def two_arrival(i, b):
+        return to_batch(r.t[i].at[0], r.u[i].at[b], r.s_twosend.at[i, 0], r.s_tworecv.at[i, b], b)
+
+    def three_copy(i, k, which, target):
+        slot = r.z[i].at[which]
+        return to_height(slot, slot, r.s_threesend.at[i, k], r.s_threerecv.at[i, which], target)
+
+    others = (twin, across, corner)
+    owned = lax.div(me, HB) == side
+
+    def stage_one(i):
+        one_copy(i, 1 - side, twin).start()
+
+    def stage_two(i):
+        one_copy(i, side, hh).wait_recv()
+
+        def add(j):
+            b = side * HB + j
+            r.t[i][j] = (r.d[i][b].astype(f32) + r.p[i][j].astype(f32)).astype(bf16)
+
+            @pl.when(b != me)
+            def _():
+                two_copy(i, j, b).start()
+
+        loop(0, HB, add)
+
+    def stage_three(i):
+        @pl.when(owned)
+        def _():
+            loop(1, B, lambda k: two_arrival(i, next_batch(k)).wait_recv())
+            r.u[i][me] = r.t[i][me - side * HB]
+            total = r.u[i][0].astype(f32)
+            for b in range(1, B):
+                total = total + r.u[i][b].astype(f32)
+            r.z[i][pair] = total.astype(r.z[i].dtype)
+            for k, target in enumerate(others):
+                three_copy(i, k, pair, target).start()
+
+    def stage_four(i):
+        @pl.when(jnp.logical_not(owned))
+        def _():
+            three_copy(i, 0, pair, hh).wait_recv()
+
+        three_copy(i, 0, 1 - pair, hh).wait_recv()
+
+    def small_one(j, half, target):
+        return to_height(r.sp[j].at[half], r.sr[j], r.s_smallsend.at[j], r.s_smallrecv.at[j], target)
+
+    def small_two(j, k):
+        slot = r.su[j].at[me]
+        return to_batch(slot, slot, r.s_smalltwo.at[j, k], r.s_smalltwor.at[j, me], next_batch(k))
+
+    def small_two_arrival(j, k):
+        b = next_batch(k)
+        slot = r.su[j].at[b]
+        return to_batch(slot, slot, r.s_smalltwo.at[j, k], r.s_smalltwor.at[j, b], b)
+
+    def small_three(j, k, which, target):
+        slot = r.sz[j].at[which]
+        return to_height(slot, slot, r.s_smallthree.at[j, k], r.s_smallthreer.at[j, which], target)
+
+    def small_stage_one(j):
+        small_one(j, 1 - side, twin).start()
+
+    def small_stage_two(j):
+        small_one(j, side, hh).wait_recv()
+        r.su[j][me] = (r.sp[j][side] + r.sr[j][...]).astype(r.su[j].dtype)
+        loop(1, B, lambda k: small_two(j, k).start())
+
+    def small_stage_three(j):
+        loop(1, B, lambda k: small_two_arrival(j, k).wait_recv())
+        total = r.su[j][0].astype(f32)
+        for b in range(1, B):
+            total = total + r.su[j][b].astype(f32)
+        r.sz[j][hh] = total
+        for k, target in enumerate(others):
+            small_three(j, k, hh, target).start()
+
+    def small_stage_four(j):
+        for other in others:
+            small_three(j, 0, other, hh).wait_recv()
+
+    stage_one(1)
 
     dkv = r.dkv
     y_lane = jnp.where(lane < 64, y_at + 2 * (KR - 1) - lane, x_at + 2 * (KC - 1) - (lane - 64))
@@ -455,14 +559,19 @@
     back_spot = jnp.where(back_ok, back_at + jnp.where(lane < 64, 64, 64 + KR), 0)
     back_ok = back_ok.astype(f32)
 
-    def dkv_copy(n, k, target):
-        return to_height(
-            dkv.at[n, pl.ds(pl.multiple_of(target * (KL * KCP), KL * KCP), KROWS), :],
-            r.dkvr.at[k - 1, n],
-            r.s_dsend.at[n, k - 1],
-            r.s_drecv.at[n, k - 1],
-            target,
-        )
+    def key_rows_of(ref, n, h):
+        return ref.at[n, pl.ds(pl.multiple_of(h * (KL * KCP), KL * KCP), KROWS), :]
+
+    def dkv_one(n, k, h, target):
+        return to_height(key_rows_of(dkv, n, h), r.dkvr.at[k, n], r.s_dsend.at[n, k], r.s_drecv.at[n, k], target)
+
+    def dkv_two(n, target):
+        return to_height(r.dkvs.at[n], r.dkvr.at[2, n], r.s_dsend.at[n, 2], r.s_drecv.at[n, 2], target)
+
+    def dkv_on(n):
+        dkv_one(n, 0, across, hh).wait_recv()
+        r.dkvs[n] = (key_rows_of(dkv, n, across)[...].astype(f32) + r.dkvr[0, n].astype(f32)).astype(bf16)
+        dkv_two(n, across).start()
 
     def attention_back(n):
         value = r.va[n]
@@ -489,8 +598,8 @@
         dkv[n, 0:KEYS, :D] = (key_grad * SCALE).astype(bf16)
         dkv[n, 0:KEYS, D:] = value_grad.astype(bf16)
         dkv[n, KEYS:, :] = jnp.zeros((dkv.shape[1] - KEYS, 2 * D), bf16)
-        for k in range(1, HG):
-            dkv_copy(n, k, next_height(k)).start()
+        dkv_one(n, 0, corner, twin).start()
+        dkv_one(n, 1, twin, twin).start()
         back = jnp.concatenate(dq + along, axis=0).T
         right = back[:, 128:]
         apart = []
@@ -506,44 +615,35 @@
         r.dqs[0, n] = outer[:HX]
         r.dqs[1, n] = outer[HX:]
 
+        @pl.when(n == 0)
+        def _():
+            stage_two(1)
+
+        @pl.when(n > 0)
+        def _():
+            dkv_on(n - 1)
+
     loop(0, IMG, attention_back)
     back_up = to_height(r.dqs.at[0], r.dqr.at[1], r.s_qsend.at[0], r.s_qrecv.at[0], above)
     back_down = to_height(r.dqs.at[1], r.dqr.at[0], r.s_qsend.at[1], r.s_qrecv.at[1], below)
     back_up.start()
     back_down.start()
 
-    def two_copy(i, j, b):
-        return to_batch(r.t[i].at[j], r.u[i].at[me], r.s_twosend.at[i, j], r.s_tworecv.at[i, me], b)
-
-    def two_arrival(i, b):
-        return to_batch(r.t[i].at[0], r.u[i].at[b], r.s_twosend.at[i, 0], r.s_tworecv.at[i, b], b)
-
-    def stage_one(i):
-        for k in range(1, HG):
-            one_copy(i, k, hh).wait_recv()
-
-        def add(j):
-            b = hh * QB + j
-            total = r.d[i][b].astype(f32)
-            for k in range(HG - 1):
-                total = total + r.p[i][k, j].astype(f32)
-            r.t[i][j] = total.astype(bf16)
-
-            @pl.when(b != me)
-            def _():
-                two_copy(i, j, b).start()
-
-        loop(0, QB, add)
-
-    stage_one(1)
-
     both = tn(flat(r.qh), flat(r.dr))
     rel = (
         both[:HD, 0:128] + both[:HD, 256:384] + both[HD:, 128:256] + both[HD:, 384:512]
     )
     rel = jnp.concatenate([rel, jnp.zeros((128 - HD, 128), f32)], axis=0).T
-    for q in range(HG):
-        r.smallp[q, 24:, :] = rel[32 * q : 32 * (q + 1)]
+    dkv_on(IMG - 1)
+    early = r.early
+    early[...] = jnp.zeros_like(early)
+    early[0:48, 0:128] = rel[0:48]
+    early[0:48, 128:256] = rel[48:96]
+    early[0:32, 256:384] = rel[96:128]
+    for i, piece in enumerate((acc[0:1, 2 * D : 3 * D], acc[0:1, 3 * D :], acc[1:2, 0:D], acc[1:2, D : 2 * D])):
+        early[48 + i : 49 + i, D:] = piece
+    early[58:59, :] = acc[2:3, : 2 * D]
+    early[59:60, :] = acc[2:3, 2 * D :]
 
     has_above = (hh > 0).astype(f32)
     has_below = (hh < HG - 1).astype(f32)
@@ -568,13 +668,21 @@
         r.pq[n] = (total * cell_mask(n)).astype(bf16)
 
     loop(0, IMG, queries_back)
+    r.f_q[...] = tn(flat(r.ne), flat(r.pq))
+    for b in range(B):
+        r.d[2][b] = r.f_q[rows * b : rows * (b + 1), :].astype(bf16)
+    stage_one(2)
+    for t in range(9):
+        early[48 + t : 49 + t, 0:D] = jnp.sum(paccq[t], axis=0, keepdims=True)
+    early[57:58, 0:D] = nn(ones, flat(r.pq))[0:1]
+    for k in range(2):
+        r.sp[0][k] = early[32 * k : 32 * (k + 1), :]
+    small_stage_one(0)
 
     def keys_values_back(n):
-        for k in range(1, HG):
-            dkv_copy(n, k, hh).wait_recv()
-        total = dkv[n, pl.ds(pl.multiple_of(hh * (KL * KCP), KL * KCP), KROWS), :].astype(f32)
-        for k in range(HG - 1):
-            total = total + r.dkvr[k, n].astype(f32)
+        dkv_one(n, 1, hh, hh).wait_recv()
+        dkv_two(n, hh).wait_recv()
+        total = key_rows_of(dkv, n, hh)[...].astype(f32) + r.dkvr[1, n].astype(f32) + r.dkvr[2, n].astype(f32)
         wide = nn(r.unpick[...], halves(total, 0))
         taps = [wide[T // 2 * a : T // 2 * (a + 1)] for a in range(3)]
         field = kvx[n]
@@ -593,13 +701,12 @@
 
     loop(0, IMG, keys_values_back)
 
-    r.f_q[...] = tn(flat(r.ne), flat(r.pq))
     r.f_kv[...] = tn(flat(r.ne), flat(r.pkv))
     for b in range(B):
-        at = slice(rows * b, rows * (b + 1))
-        r.d[0][b] = jnp.concatenate([r.f_q[at, :], r.f_kv[at, :]], axis=1).astype(bf16)
-    for k in range(1, HG):
-        one_copy(0, k, next_height(k)).start()
+        r.d[0][b] = r.f_kv[rows * b : rows * (b + 1), :].astype(bf16)
+    stage_one(0)
+    stage_two(2)
+    small_stage_two(0)
 
     def projection_back(n):
         grad = nt(r.pq[n], wq[...]) + nt(r.pkv[n], wkv[...])
@@ -608,123 +715,78 @@
         acc[0:1, D : 2 * D] += jnp.sum(grad, axis=0, keepdims=True)
         r.v_ig[n] = r.mgd[n] + normalise_back(grad, gain_one, hat, r.inv_one[n])
 
+        @pl.when(n == 0)
+        def _():
+            stage_two(0)
+
     loop(0, IMG, projection_back)
     input_out = pltpu.make_async_copy(r.v_ig, r.o_ig, r.s_out.at[1])
     input_out.start()
 
-    small = r.small
-    small[...] = jnp.zeros_like(small)
+    late = r.late
+    late[...] = jnp.zeros_like(late)
     for t in range(9):
-        small[t : t + 1, 0:D] = jnp.sum(paccq[t], axis=0, keepdims=True)
-        small[t : t + 1, D : 3 * D] = jnp.sum(pacckv[t], axis=0, keepdims=True)
-    small[9:10, 0:D] = nn(ones, flat(r.pq))[0:1]
-    small[9:10, D : 3 * D] = nn(ones, flat(r.pkv))[0:1]
-    small[10:13, :] = acc[...]
-    for q in range(HG):
-        for i in range(6):
-            r.smallp[q, 4 * i : 4 * (i + 1), :] = small[4 * q : 4 * (q + 1), 128 * i : 128 * (i + 1)]
-
-    def small_one(k, target):
-        return to_height(
-            r.smallp.at[target], r.smallr.at[k - 1], r.s_smallsend.at[k - 1], r.s_smallrecv.at[k - 1], target
-        )
-
-    for k in range(1, HG):
-        small_one(k, next_height(k)).start()
-
-    def small_two(k):
-        slot = r.smallu.at[me]
-        return to_batch(slot, slot, r.s_smalltwo.at[k], r.s_smalltwor.at[me], next_batch(k))
-
-    def small_two_arrival(k):
-        b = next_batch(k)
-        slot = r.smallu.at[b]
-        return to_batch(slot, slot, r.s_smalltwo.at[k], r.s_smalltwor.at[b], b)
-
-    stage_one(0)
-    for k in range(1, HG):
-        small_one(k, hh).wait_recv()
-    total = r.smallp[hh]
-    for k in range(HG - 1):
-        total = total + r.smallr[k]
-    r.smallu[me] = total
-    loop(1, B, lambda k: small_two(k).start())
-
-    owned = me // QB == hh
-    spans = (slice(PE, PE + PI), slice(0, PE))
-
-    def three_copy(i, k):
-        return to_height(
-            r.z[i], r.z[i], r.s_threesend.at[i, k - 1], r.s_threerecv.at[i], next_height(k)
-        )
-
-    @pl.when(owned)
-    def _():
-        for i in (1, 0):
-            loop(1, B, lambda k, i=i: two_arrival(i, next_batch(k)).wait_recv())
-            r.u[i][me] = r.t[i][me - hh * QB]
-            total = r.u[i][0].astype(f32)
-            for b in range(1, B):
-                total = total + r.u[i][b].astype(f32)
-            r.z[i][...] = total
-            for k in range(1, HG):
-                three_copy(i, k).start()
-
-    def small_three(k):
-        slot = r.smallz.at[hh]
-        return to_height(slot, slot, r.s_smallthree.at[k - 1], r.s_smallthreer.at[k - 1], next_height(k))
-
-    def small_three_arrival(k):
-        slot = r.smallz.at[next_height(HG - k)]
-        return to_height(slot, slot, r.s_smallthree.at[k - 1], r.s_smallthreer.at[k - 1], next_height(k))
-
-    loop(1, B, lambda k: small_two_arrival(k).wait_recv())
-    total = r.smallu[0]
-    for b in range(1, B):
-        total = total + r.smallu[b]
-    r.smallz[hh] = total
-    for k in range(1, HG):
-        small_three(k).start()
-
-    @pl.when(jnp.logical_not(owned))
-    def _():
-        for i in range(2):
-            three_copy(i, 1).wait_recv()
-
-    for k in range(1, HG):
-        small_three_arrival(k).wait_recv()
-    outs = [(r.z[0], r.o_z[0]), (r.z[1], r.o_z[1]), (r.smallz, r.o_small)]
+        late[t : t + 1, :] = jnp.sum(pacckv[t], axis=0, keepdims=True)
+    late[9:10, :] = nn(ones, flat(r.pkv))[0:1]
+    late[10:11, :] = acc[0:1, 0 : 2 * D]
+    for k in range(2):
+        r.sp[1][k] = late[8 * k : 8 * (k + 1), :]
+    small_stage_one(1)
+    stage_three(1)
+    small_stage_two(1)
+    stage_three(2)
+    small_stage_three(0)
+    stage_three(0)
+    small_stage_three(1)
+    for i in (1, 2, 0):
+        stage_four(i)
+    for j in range(2):
+        small_stage_four(j)
+    outs = list(zip(r.z, r.o_z)) + list(zip(r.sz, r.o_sz))
     outs = [pltpu.make_async_copy(a, b, r.s_out.at[2 + k]) for k, (a, b) in enumerate(outs)]
     for out in outs:
         out.start()
 
-    for copy in (halo_up, halo_down, back_up, back_down):
+    for copy in (halo_up, halo_down, back_up, back_down, rest_handed(side, twin)):
         copy.wait_send()
-    for i in range(2):
-        loop(1, B, lambda k, i=i: weight_copy(i, k).wait_send())
-    for k in range(1, HG):
-        for n in range(IMG):
-            kv_copy(n, k, hh, next_height(k)).wait_send()
-            dkv_copy(n, k, next_height(k)).wait_send()
-        for i in range(2):
-            one_copy(i, k, next_height(k)).wait_send()
-        small_one(k, next_height(k)).wait_send()
-        small_three(k).wait_send()
+
+    def sent_weights(k):
+        in_copy(k).wait_send()
+        rest_copy(k).wait_send()
+        for j in range(2):
+            small_two(j, k).wait_send()
+
+    loop(1, B, sent_weights)
+
+    def sent_images(n):
+        kv_copy(n, 0, hh, twin).wait_send()
+        kv_copy(n, 1, hh, across).wait_send()
+        kv_copy(n, 2, across, twin).wait_send()
+        dkv_one(n, 0, corner, twin).wait_send()
+        dkv_one(n, 1, twin, twin).wait_send()
+        dkv_two(n, across).wait_send()
+
+    loop(0, IMG, sent_images)
+    for i in range(3):
+        one_copy(i, 1 - side, twin).wait_send()
+    for j in range(2):
+        small_one(j, 1 - side, twin).wait_send()
+        for k, target in enumerate(others):
+            small_three(j, k, hh, target).wait_send()
 
     def sent_two(j):
-        @pl.when(hh * QB + j != me)
+        @pl.when(side * HB + j != me)
         def _():
-            for i in range(2):
-                two_copy(i, j, hh * QB + j).wait_send()
-
-    loop(0, QB, sent_two)
-    loop(1, B, lambda k: small_two(k).wait_send())
+            for i in range(3):
+                two_copy(i, j, side * HB + j).wait_send()
+
+    loop(0, HB, sent_two)
 
     @pl.when(owned)
     def _():
-        for i in range(2):
-            for k in range(1, HG):
-                three_copy(i, k).wait_send()
+        for i in range(3):
+            for k, target in enumerate(others):
+                three_copy(i, k, pair, target).wait_send()
 
     result_out.wait()
     input_out.wait()
@@ -751,35 +813,44 @@
     for index, (source, target) in enumerate(zip(r.given, r.v_given)):
         arrivals.append(pltpu.make_async_copy(source, row(target), r.s_in.at[index]))
         arrivals[-1].start()
-    rows = r.v_given[0].shape[0]
-    small = r.small
-    for i in range(4):
+    through = [(r.ig, r.v_ig, r.o_ig), (r.res, r.v_res, r.o_res)]
+    through = [
+        (pltpu.make_async_copy(a, b, r.s_through.at[k]), pltpu.make_async_copy(b, c, r.s_through.at[2 + k]))
+        for k, (a, b, c) in enumerate(through)
+    ]
+    for enter, _ in through:
+        enter.start()
+    for i in range(5):
         arrivals[i].wait()
-    for q in range(HG):
-        for i in range(6):
-            small[4 * q : 4 * (q + 1), 128 * i : 128 * (i + 1)] = r.v_given[2][q, 4 * i : 4 * (i + 1), :]
-    rel = jnp.concatenate([r.v_given[2][q, 24:, :] for q in range(HG)], axis=0)
+    planes = [x[0].astype(f32) + x[1].astype(f32) for x in r.v_given[0:3]]
+    early, late = [
+        jnp.concatenate([x[0] + x[2], x[1] + x[3]], axis=0) for x in r.v_given[3:5]
+    ]
+    pack = planes[1]
+    rel = jnp.concatenate([early[0:48, 0:128], early[0:48, 128:256], early[0:32, 256:384]], axis=0)
     for t in range(9):
-        for i in range(3):
-            r.pgrad[t, i : i + 1, :] = small[t : t + 1, D * i : D * (i + 1)]
+        r.pgrad[t, 0:1, :] = early[48 + t : 49 + t, 0:D]
+        r.pgrad[t, 1:2, :] = late[t : t + 1, 0:D]
+        r.pgrad[t, 2:3, :] = late[t : t + 1, D:]
     bgrad = r.bgrad
-    bgrad[0:1, 0:D] = small[10:11, D : 2 * D]
-    bgrad[0:1, D : 2 * D] = small[10:11, 3 * D :]
-    bgrad[0:1, 2 * D : 5 * D] = small[9:10, : 3 * D]
-    bgrad[0:1, 5 * D : 6 * D] = small[11:12, 0:D]
-    bgrad[0:1, 6 * D : 6 * D + HID] = small[12:13, :]
-    bgrad[0:1, 6 * D + HID :] = small[11:12, D : 2 * D]
-    pack = r.v_given[1]
-    given = [r.v_given[3 + 3 * index : 6 + 3 * index] for index in range(9)]
+    bgrad[0:1, 0:D] = late[10:11, D:]
+    bgrad[0:1, D : 2 * D] = early[49:50, D:]
+    bgrad[0:1, 2 * D : 3 * D] = early[57:58, 0:D]
+    bgrad[0:1, 3 * D : 5 * D] = late[9:10, :]
+    bgrad[0:1, 5 * D : 6 * D] = early[50:51, D:]
+    bgrad[0:1, 6 * D : 8 * D] = early[58:59, :]
+    bgrad[0:1, 8 * D : 10 * D] = early[59:60, :]
+    bgrad[0:1, 10 * D :] = early[51:52, D:]
+    given = [r.v_given[5 + 3 * index : 8 + 3 * index] for index in range(9)]
     gradients = [
-        lambda: r.v_given[0][...],
-        lambda: pack[:, HID + 4 * D : HID + 5 * D],
+        lambda: jnp.concatenate([planes[2], planes[0]], axis=1),
+        lambda: jnp.concatenate([pack[:, HID:PH], pack[:, PH + 4 * D : PH + 5 * D - 128]], axis=1),
         lambda: pack[:, :HID],
-        lambda: jnp.concatenate([pack[:, HID + D * i : HID + D * (i + 1)] for i in range(4)], axis=0),
+        lambda: jnp.concatenate([pack[:, PH + D * i : PH + D * (i + 1)] for i in range(4)], axis=0),
         lambda: r.pgrad[...],
         lambda: rel[0 : given[5][0].shape[0], 0:HD],
         lambda: rel[64 : 64 + given[6][0].shape[0], 0:HD],
-        lambda: jnp.concatenate([small[10:11, 0:D], small[10:11, 2 * D : 3 * D]], axis=0),
+        lambda: jnp.concatenate([late[10:11, 0:D], early[48:49, D:]], axis=0),
         lambda: bgrad[...],
     ]
     leaving = []
@@ -791,8 +862,7 @@
 
     for index in range(9):
         for k in range(3):
-            if index or k:
-                arrivals[3 + 3 * index + k].wait()
+            arrivals[5 + 3 * index + k].wait()
         weight, first, second = [x[...] for x in given[index]]
         fresh = adam_step(
             weight, first, second, gradients[index](), step_rates[index], decay_rates[index]
@@ -803,6 +873,11 @@
         for k, value in enumerate(fresh):
             r.v_fresh[at + k][...] = value
             leave(at + k)
+        if index == 0:
+            for enter, leave_again in through:
+                enter.wait()
+                leave_again.start()
+                leaving.append(leave_again)
     for copy in leaving:
         copy.wait()
 
@@ -815,7 +890,7 @@
         params[k] = params[k].transpose(1, 0, 2)
     weights = params[0::3]
     rows = weights[0].shape[0]
-    QB = B // HG
+    HB = B // 2
     assert weights[3].shape[0] == 4 * rows
 
     def by_column(x):
@@ -864,10 +939,10 @@
     results = dict(
         o_res=jax.ShapeDtypeStruct((IMG, T, D), bf16),
         o_ig=jax.ShapeDtypeStruct((IMG, T, D), f32),
-        o_z=[jax.ShapeDtypeStruct((rows, PI), f32), jax.ShapeDtypeStruct((rows, PE), f32)],
-        o_small=jax.ShapeDtypeStruct((HG, 56, 128), f32),
+        o_z=[jax.ShapeDtypeStruct((2, rows, x), y) for x, y in ((2 * D, f32), (PE, bf16), (D, f32))],
+        o_sz=[jax.ShapeDtypeStruct((HG, x, 2 * D), f32) for x in (32, 8)],
     )
-    lanes = (PI, PE)
+    lanes = (2 * D, PE, D)
     scratch = dict(
         v_act=vm((IMG, T, D), bf16),
         v_cot=vm((IMG, T, D), bf16),
@@ -880,12 +955,19 @@
         v_relw=vm(weights[6].shape, f32),
         v_gains=vm(weights[7].shape, f32),
         v_biases=vm((1,) + weights[8].shape, f32),
-        g=[vm((B, rows, x), bf16) for x in lanes],
+        gin=vm((B, rows, 3 * D), bf16),
+        grest=vm((2, B, rows, PH), bf16),
         d=[vm((B, rows, x), bf16) for x in lanes],
-        p=[vm((HG - 1, QB, rows, x), bf16) for x in lanes],
-        t=[vm((QB, rows, x), bf16) for x in lanes],
+        p=[vm((HB, rows, x), bf16) for x in lanes],
+        t=[vm((HB, rows, x), bf16) for x in lanes],
         u=[vm((B, rows, x), bf16) for x in lanes],
-        z=[vm((rows, x), f32) for x in lanes],
+        z=[vm(x.shape, x.dtype) for x in results["o_z"]],
+        sp=[vm((2, x, 2 * D), f32) for x in (32, 8)],
+        sr=[vm((x, 2 * D), f32) for x in (32, 8)],
+        su=[vm((B, 32, 2 * D), bf16), vm((B, 8, 2 * D), f32)],
+        sz=[vm(x.shape, x.dtype) for x in results["o_sz"]],
+        early=vm((64, 2 * D), f32),
+        late=vm((16, 2 * D), f32),
         f_q=vm((D, D), f32),
         f_kv=vm((D, 2 * D), f32),
         f_exp=vm((D, HID), f32),
@@ -936,41 +1018,37 @@
         v_res=vm((IMG, T, D), bf16),
         v_ig=vm((IMG, T, D), f32),
         dkv=vm((IMG, KEYS + KL * KCP, 2 * D), bf16),
-        dkvr=vm((HG - 1, IMG, KROWS, 2 * D), bf16),
+        dkvr=vm((3, IMG, KROWS, 2 * D), bf16),
+        dkvs=vm((IMG, KROWS, 2 * D), bf16),
         dqs=vm((2, IMG, HX, D), bf16),
         dqr=vm((2, IMG, HX, D), bf16),
         dr=vm((IMG, T, 512), bf16),
         pq=vm((IMG, T, D), bf16),
         pkv=vm((IMG, T, 2 * D), bf16),
-        small=vm((16, HID), f32),
-        smallp=vm((HG, 56, 128), f32),
-        smallr=vm((HG - 1, 56, 128), f32),
-        smallu=vm((B, 56, 128), f32),
-        smallz=vm((HG, 56, 128), f32),
         s_local=dma((11,)),
-        s_out=dma((5,)),
+        s_out=dma((7,)),
         s_wsend=dma((2, B)),
-        s_wrecv=dma((2, B)),
+        s_wrecv=dma((3, B)),
         s_hsend=dma((2,)),
         s_hrecv=dma((2,)),
-        s_ksend=dma((IMG, HG - 1)),
-        s_krecv=dma((IMG, HG - 1)),
-        s_dsend=dma((IMG, HG - 1)),
-        s_drecv=dma((IMG, HG - 1)),
+        s_ksend=dma((IMG, 3)),
+        s_krecv=dma((IMG, 3)),
+        s_dsend=dma((IMG, 3)),
+        s_drecv=dma((IMG, 3)),
         s_qsend=dma((2,)),
         s_qrecv=dma((2,)),
-        s_onesend=dma((2, HG - 1)),
-        s_onerecv=dma((2, HG - 1)),
-        s_smallsend=dma((HG - 1,)),
-        s_smallrecv=dma((HG - 1,)),
-        s_twosend=dma((2, QB)),
-        s_tworecv=dma((2, B)),
-        s_smalltwo=dma((B,)),
-        s_smalltwor=dma((B,)),
-        s_threesend=dma((2, HG - 1)),
-        s_threerecv=dma((2,)),
-        s_smallthree=dma((HG - 1,)),
-        s_smallthreer=dma((HG - 1,)),
+        s_onesend=dma((3,)),
+        s_onerecv=dma((3,)),
+        s_twosend=dma((3, HB)),
+        s_tworecv=dma((3, B)),
+        s_threesend=dma((3, 3)),
+        s_threerecv=dma((3, 2)),
+        s_smallsend=dma((2,)),
+        s_smallrecv=dma((2,)),
+        s_smalltwo=dma((2, B)),
+        s_smalltwor=dma((2, B)),
+        s_smallthree=dma((2, 3)),
+        s_smallthreer=dma((2, HG)),
     )
     main = call(
         functools.partial(main_kernel, B),
@@ -979,11 +1057,11 @@
         scratch,
         {id(operands["extent"]): pl.BlockSpec(memory_space=pltpu.SMEM)},
         compiler_params=pltpu.CompilerParams(
-            collective_id=0, has_side_effects=True, vmem_limit_bytes=52 * 1024 * 1024
+            collective_id=0, has_side_effects=True, vmem_limit_bytes=60 * 1024 * 1024
         ),
         name="block",
     )
-    given = main["o_z"] + [main["o_small"]] + params
+    given = main["o_z"] + main["o_sz"] + params
     fresh = []
     for index in range(9):
         fresh += [like(weights[index]) for _ in range(3)]
@@ -995,27 +1073,30 @@
 
     fresh = call(
         adam_kernel,
-        dict(given=given),
-        dict(fresh=fresh),
+        dict(given=given, res=main["o_res"], ig=main["o_ig"]),
+        dict(fresh=fresh, o_res=like(main["o_res"]), o_ig=like(main["o_ig"])),
         dict(
             v_given=[room(x) for x in given],
             v_fresh=[room(x) for x in fresh],
-            small=vm((16, HID), f32),
             pgrad=vm(weights[4].shape, f32),
             bgrad=vm((1,) + weights[8].shape, f32),
             s_in=dma((len(given),)),
             s_out=dma((len(fresh),)),
+            s_through=dma((4,)),
+            v_res=vm((IMG, T, D), bf16),
+            v_ig=vm((IMG, T, D), f32),
         ),
         {},
         name="adam",
-    )["fresh"]
+    )
+    res, ig, fresh = fresh["o_res"], fresh["o_ig"], fresh["fresh"]
     for k in range(16, 19):
         fresh[k] = fresh[k].transpose(1, 0, 2)
 
     def by_row(x):
         return x.reshape(IMG, C, R, D).transpose(0, 2, 1, 3)
 
-    return (by_row(main["o_res"]), by_row(main["o_ig"])) + tuple(fresh)
+    return (by_row(res), by_row(ig)) + tuple(fresh)
 
 
 def solution(mesh):

time: 89.1 us -> 62.7 us (0.70)
  the two profiles are of different devices: /device:TPU:25 before, /device:TPU:0 now
where the time goes in v2:
time: 62.7 us; the launch traced here: 62.2 us
  Pallas kernels  61.5 us (98%)
  between operations  0.69 us (1%)
    pallas_call x2, Pallas kernels, call(): pl.pallas_call(ordered, out_shape=flat_results, in_specs=[specs.get(id(x)...  61.5 us

profile of v2, /device:TPU:0, one launch (start us, length us, event | category | flops | bytes accessed | tf_op | source)
XLA Modules:
  0.0 62.2 jit_solution(7482890487063437987)
XLA Ops:
  0.7 57.8 %block.1 = (f32[3,224,192]{2,1,0:T(8,128)}, bf16[3,224,192]{2,1,0:T(8,128)(2,1)}, f32[4,32,384]{2,1,0:T(8,128)}, f32[4,8,384]{2,1,0:T(8,128)}, f32[2,24,384]{2,1...) custom-call(bf16[3,224,192]{2,1,0:T(8,128)(2,1)} %bitcast.19, f32[2112]{0:T(1024)} %refs_29_.1, ...), custom_call_target="tpu_custom_call" | custom-call | tf_op jit(solution)/shard_map/block/pallas_call | solution.py:915
  58.4 3.8 %adam.1 = (f32[24,576]{1,0:T(8,128)}, f32[24,576]{1,0:T(8,128)}, f32[24,576]{1,0:T(8,128)}, bf16[24,576]{1,0:T(8,128)(2,1)}, f32[24,192]{1,0:T(8,128)}, /*index=...) custom-call(f32[2,24,384]{2,1,0:T(8,128)} %get-tuple-element.73.refs, ...), custom_call_target="tpu_custom_call" | custom-call | tf_op jit(solution)/shard_map/adam/pallas_call | solution.py:915

commit v3 on v2

--- a/solution.py
+++ b/solution.py
@@ -139,35 +139,46 @@
             src_ref=src, dst_ref=dst, send_sem=send, recv_sem=recv, device_id=(me, h), device_id_type=MESH
         )
 
-    def in_copy(k):
-        slot = r.gin.at[me]
-        return to_batch(slot, slot, r.s_wsend.at[0, k], r.s_wrecv.at[0, me], next_batch(k))
-
-    def in_arrival(k):
+    def in_slot(i, b):
+        return r.gkv.at[side, b] if i == 0 else r.gq_in.at[b]
+
+    def in_copy(i, k):
+        slot = in_slot(i, me)
+        return to_batch(slot, slot, r.s_isend.at[i, k], r.s_irecv.at[i, me], next_batch(k))
+
+    def in_arrival(i, k):
         b = next_batch(k)
-        slot = r.gin.at[b]
-        return to_batch(slot, slot, r.s_wsend.at[0, k], r.s_wrecv.at[0, b], b)
+        slot = in_slot(i, b)
+        return to_batch(slot, slot, r.s_isend.at[i, k], r.s_irecv.at[i, b], b)
+
+    def in_handed(half, target):
+        slot = r.gkv.at[half]
+        return to_height(slot, slot, r.s_hand.at[2], r.s_hand.at[3], target)
 
     def rest_copy(k):
         slot = r.grest.at[side, me]
-        return to_batch(slot, slot, r.s_wsend.at[1, k], r.s_wrecv.at[1, me], next_batch(k))
+        return to_batch(slot, slot, r.s_wsend.at[k], r.s_wrecv.at[me], next_batch(k))
 
     def rest_arrival(k):
         b = next_batch(k)
         slot = r.grest.at[side, b]
-        return to_batch(slot, slot, r.s_wsend.at[1, k], r.s_wrecv.at[1, b], b)
+        return to_batch(slot, slot, r.s_wsend.at[k], r.s_wrecv.at[b], b)
 
     def rest_handed(half, target):
         slot = r.grest.at[half]
-        return to_height(slot, slot, r.s_wsend.at[0, 0], r.s_wrecv.at[2, 0], target)
-
-    local[0].wait()
+        return to_height(slot, slot, r.s_hand.at[0], r.s_hand.at[1], target)
+
     local[1].wait()
-    r.gin[me] = r.v_in[...].astype(bf16)
+    r.gkv[side, me] = jnp.where(side == 0, r.v_in[:, D : 2 * D], r.v_in[:, 2 * D :]).astype(bf16)
+    r.gq_in[me] = r.v_in[:, :D].astype(bf16)
+    pl.semaphore_wait(barrier, B - 1 + HG - 1)
+    loop(1, B, lambda k: in_copy(0, k).start())
+    loop(1, B, lambda k: in_copy(1, k).start())
 
     edge_rows = iota((2 * HX, T), 0)
     edge_cols = iota((2 * HX, T), 1)
     edges = (edge_cols == (edge_rows % HX) * R + (edge_rows // HX) * (R - 1)).astype(bf16)
+    local[0].wait()
     for n in range(IMG):
         outer = nn(edges, r.v_act[n]).astype(bf16)
         r.hs[0, n] = outer[:HX]
@@ -176,8 +187,6 @@
     halo_up = to_height(r.hs.at[0], r.hr.at[1], r.s_hsend.at[0], r.s_hrecv.at[0], above)
     halo_down = to_height(r.hs.at[1], r.hr.at[0], r.s_hsend.at[1], r.s_hrecv.at[1], below)
 
-    pl.semaphore_wait(barrier, B - 1 + HG - 1)
-    loop(1, B, lambda k: in_copy(k).start())
     halo_up.start()
     halo_down.start()
     for k in (2, 3, 4):
@@ -234,7 +243,8 @@
             x[n, 0:R, :] = jnp.zeros((R, D), f32)
             x[n, T + R :, :] = jnp.zeros((R, D), f32)
 
-    loop(0, IMG, first_norm)
+    for n in range(IMG):
+        first_norm(n)
 
     spread_rows = iota((T, 2 * HX), 0)
     spread_cols = iota((T, 2 * HX), 1)
@@ -278,13 +288,14 @@
         )
     halo_ok = halo_ok.astype(f32)
 
-    loop(1, B, lambda k: in_arrival(k).wait_recv())
     wq, wkv, wout, wexp, wred = r.wq, r.wkv, r.wout, r.wexp, r.wred
+
+    loop(1, B, lambda k: in_arrival(0, k).wait_recv())
+    in_handed(side, twin).start()
+    in_handed(1 - side, hh).wait_recv()
     for b in range(B):
-        shard = r.gin[b].astype(f32)
-        r.f_q[rows * b : rows * (b + 1), :] = shard[:, :D]
-        r.f_kv[rows * b : rows * (b + 1), :] = shard[:, D:]
-    wq[...] = r.f_q[...].astype(bf16)
+        for i in range(2):
+            r.f_kv[rows * b : rows * (b + 1), D * i : D * (i + 1)] = r.gkv[i, b].astype(f32)
     wkv[...] = r.f_kv[...].astype(bf16)
 
     kvg = r.kvg
@@ -318,8 +329,13 @@
         kv_copy(n, 1, hh, across).start()
         kv_copy(n, 0, hh, twin).start()
 
-    loop(0, IMG, keys_values)
-
+    for n in range(IMG):
+        keys_values(n)
+
+    loop(1, B, lambda k: in_arrival(1, k).wait_recv())
+    for b in range(B):
+        r.f_q[rows * b : rows * (b + 1), :] = r.gq_in[b].astype(f32)
+    wq[...] = r.f_q[...].astype(bf16)
     qp, qa = r.qp, r.qa
     r.halo_q[...] = (nn(r.nh[...], wq[...]) + bias_q) * halo_ok
     lane = iota((T, 128), 1)
@@ -364,15 +380,15 @@
                 qa[n, hd, :, :128] = jnp.where(lane < HD, 0.0, left).astype(bf16)
                 qa[n, hd, :, 128:] = jnp.where(lane < 64, right, near).astype(bf16)
 
-    loop(0, IMG, queries)
+    for n in range(IMG):
+        queries(n)
 
     def kv_on(n):
         kv_copy(n, 1, across, hh).wait_recv()
         kv_copy(n, 2, across, twin).start()
 
-    loop(0, IMG, kv_on)
-    loop(1, B, lambda k: rest_arrival(k).wait_recv())
-    rest_handed(side, twin).start()
+    for n in range(IMG):
+        kv_on(n)
 
     key_at = iota((KEYS, 1), 0)
     probs, mxh = r.probs, r.mxh
@@ -396,7 +412,11 @@
             mixed.append(nn(value[HD * hd : HD * (hd + 1)], prob.astype(bf16)))
         mxh[n] = (jnp.concatenate(mixed, axis=0).T + qp[n]).astype(bf16)
 
-    loop(0, IMG, attention)
+    for n in range(IMG):
+        attention(n)
+        if n == 1:
+            loop(1, B, lambda k: rest_arrival(k).wait_recv())
+            rest_handed(side, twin).start()
 
     rest_handed(1 - side, hh).wait_recv()
     for b in range(B):
@@ -437,7 +457,8 @@
         r.ag[n] = attn_grad
         r.mg[n] = nt(attn_grad, wout[...]).astype(bf16)
 
-    loop(0, IMG, feed_forward)
+    for n in range(IMG):
+        feed_forward(n)
     result_out = pltpu.make_async_copy(r.v_res, r.o_res, r.s_out.at[0])
     result_out.start()
 
@@ -471,9 +492,11 @@
     def two_arrival(i, b):
         return to_batch(r.t[i].at[0], r.u[i].at[b], r.s_twosend.at[i, 0], r.s_tworecv.at[i, b], b)
 
+    def three_own(i):
+        return pltpu.make_async_copy(r.z[i].at[pair], r.o_z[i].at[pair], r.s_three.at[i])
+
     def three_copy(i, k, which, target):
-        slot = r.z[i].at[which]
-        return to_height(slot, slot, r.s_threesend.at[i, k], r.s_threerecv.at[i, which], target)
+        return to_height(r.z[i].at[which], r.o_z[i].at[which], r.s_threesend.at[i, k], r.s_threerecv.at[i, which], target)
 
     others = (twin, across, corner)
     owned = lax.div(me, HB) == side
@@ -505,6 +528,7 @@
             r.z[i][pair] = total.astype(r.z[i].dtype)
             for k, target in enumerate(others):
                 three_copy(i, k, pair, target).start()
+            three_own(i).start()
 
     def stage_four(i):
         @pl.when(jnp.logical_not(owned))
@@ -513,8 +537,11 @@
 
         three_copy(i, 0, 1 - pair, hh).wait_recv()
 
-    def small_one(j, half, target):
-        return to_height(r.sp[j].at[half], r.sr[j], r.s_smallsend.at[j], r.s_smallrecv.at[j], target)
+    def early_one(k, part, target):
+        return to_height(r.sp[0].at[part], r.sr[0].at[k - 1], r.s_earlysend.at[k - 1], r.s_earlyrecv.at[k - 1], target)
+
+    def late_one(half, target):
+        return to_height(r.sp[1].at[half], r.sr[1].at[0], r.s_late.at[0], r.s_late.at[1], target)
 
     def small_two(j, k):
         slot = r.su[j].at[me]
@@ -525,16 +552,36 @@
         slot = r.su[j].at[b]
         return to_batch(slot, slot, r.s_smalltwo.at[j, k], r.s_smalltwor.at[j, b], b)
 
+    def small_own(j):
+        return pltpu.make_async_copy(r.sz[j].at[hh], r.o_sz[j].at[hh], r.s_smallown.at[j])
+
     def small_three(j, k, which, target):
-        slot = r.sz[j].at[which]
-        return to_height(slot, slot, r.s_smallthree.at[j, k], r.s_smallthreer.at[j, which], target)
+        return to_height(r.sz[j].at[which], r.o_sz[j].at[which], r.s_smallthree.at[j, k], r.s_smallthreer.at[j, which], target)
 
     def small_stage_one(j):
-        small_one(j, 1 - side, twin).start()
+        if j == 0:
+            for k in range(1, HG):
+                early_one(k, next_height(k), next_height(k)).start()
+        else:
+            late_one(1 - side, twin).start()
+
+    def small_stage_one_sent(j):
+        if j == 0:
+            for k in range(1, HG):
+                early_one(k, next_height(k), next_height(k)).wait_send()
+        else:
+            late_one(1 - side, twin).wait_send()
 
     def small_stage_two(j):
-        small_one(j, side, hh).wait_recv()
-        r.su[j][me] = (r.sp[j][side] + r.sr[j][...]).astype(r.su[j].dtype)
+        if j == 0:
+            total = r.sp[0][hh]
+            for k in range(1, HG):
+                early_one(k, hh, hh).wait_recv()
+                total = total + r.sr[0][k - 1]
+        else:
+            late_one(side, hh).wait_recv()
+            total = r.sp[1][side] + r.sr[1][0]
+        r.su[j][me] = total.astype(bf16)
         loop(1, B, lambda k: small_two(j, k).start())
 
     def small_stage_three(j):
@@ -545,6 +592,7 @@
         r.sz[j][hh] = total
         for k, target in enumerate(others):
             small_three(j, k, hh, target).start()
+        small_own(j).start()
 
     def small_stage_four(j):
         for other in others:
@@ -573,33 +621,43 @@
         r.dkvs[n] = (key_rows_of(dkv, n, across)[...].astype(f32) + r.dkvr[0, n].astype(f32)).astype(bf16)
         dkv_two(n, across).start()
 
-    def attention_back(n):
+    def halo_back(n, k, target):
+        return to_height(
+            r.dqs.at[k, n], r.dqr.at[1 - k, n], r.s_qsend.at[n, k], r.s_qrecv.at[n, 1 - k], target
+        )
+
+    head = iota((T, D), 1) < HD
+
+    def heads(x):
+        x = x.astype(f32)
+        return [jnp.where(head, x, 0.0).astype(bf16), jnp.where(head, 0.0, x).astype(bf16)]
+
+    def scores_back(n):
         value = r.va[n]
-        keys = r.ka[n].T
-        mixed_grad = r.mg[n].astype(f32)
-        query = r.qh[n].astype(f32)
-        head = iota((T, D), 1) < HD
-        probs_half, grads_half, dq, along = [], [], [], []
-        mixed_heads = [jnp.where(head, mixed_grad, 0.0), jnp.where(head, 0.0, mixed_grad)]
-        mixed_heads = [x.astype(bf16) for x in mixed_heads]
-        query_heads = [jnp.where(head, query, 0.0), jnp.where(head, 0.0, query)]
-        query_heads = [x.astype(bf16) for x in query_heads]
+        mixed_heads, query_heads = heads(r.mg[n]), heads(r.qh[n])
         key_grad, value_grad = 0.0, 0.0
         for hd in range(2):
             prob = probs[n, hd]
             prob_grad = nt(value, mixed_heads[hd])
             inner = jnp.sum(prob * prob_grad, axis=0, keepdims=True)
             score_grad = (prob * (prob_grad - inner)).astype(bf16)
+            r.sg[n, hd] = score_grad
             value_grad = value_grad + nn(prob.astype(bf16), mixed_heads[hd])
             key_grad = key_grad + nn(score_grad, query_heads[hd])
-            back = nn(jnp.concatenate([keys[HD * hd : HD * (hd + 1)], keys[D : D + 32]], axis=0), score_grad)
-            dq.append(back[:HD])
-            along.append(back[HD:])
         dkv[n, 0:KEYS, :D] = (key_grad * SCALE).astype(bf16)
         dkv[n, 0:KEYS, D:] = value_grad.astype(bf16)
         dkv[n, KEYS:, :] = jnp.zeros((dkv.shape[1] - KEYS, 2 * D), bf16)
         dkv_one(n, 0, corner, twin).start()
         dkv_one(n, 1, twin, twin).start()
+
+    def rows_back(n):
+        keys = r.ka[n].T
+        dq, along = [], []
+        for hd in range(2):
+            here = jnp.concatenate([keys[HD * hd : HD * (hd + 1)], keys[D : D + 32]], axis=0)
+            back = nn(here, r.sg[n, hd])
+            dq.append(back[:HD])
+            along.append(back[HD:])
         back = jnp.concatenate(dq + along, axis=0).T
         right = back[:, 128:]
         apart = []
@@ -610,47 +668,48 @@
         apart = halves(jnp.concatenate(apart, axis=1), 1)
         r.dr[n] = apart
         from_tables = nn(apart, jnp.concatenate([table[...], table[...]], axis=0))
-        dqx[n, R : R + T, :] = back[:, :D] * SCALE + from_tables + mixed_grad
+        dqx[n, R : R + T, :] = back[:, :D] * SCALE + from_tables + r.mg[n].astype(f32)
         outer = nn(edges, dqx[n, R : R + T, :].astype(bf16)).astype(bf16)
         r.dqs[0, n] = outer[:HX]
         r.dqs[1, n] = outer[HX:]
-
-        @pl.when(n == 0)
-        def _():
-            stage_two(1)
-
-        @pl.when(n > 0)
-        def _():
-            dkv_on(n - 1)
-
-    loop(0, IMG, attention_back)
-    back_up = to_height(r.dqs.at[0], r.dqr.at[1], r.s_qsend.at[0], r.s_qrecv.at[0], above)
-    back_down = to_height(r.dqs.at[1], r.dqr.at[0], r.s_qsend.at[1], r.s_qrecv.at[1], below)
-    back_up.start()
-    back_down.start()
+        halo_back(n, 0, above).start()
+        halo_back(n, 1, below).start()
+
+    scores_back(0)
+    scores_back(1)
+    dkv_on(0)
+    scores_back(2)
+    dkv_on(1)
+    stage_two(1)
+    rows_back(0)
+    rows_back(1)
+    dkv_on(2)
+    rows_back(2)
 
     both = tn(flat(r.qh), flat(r.dr))
     rel = (
         both[:HD, 0:128] + both[:HD, 256:384] + both[HD:, 128:256] + both[HD:, 384:512]
     )
     rel = jnp.concatenate([rel, jnp.zeros((128 - HD, 128), f32)], axis=0).T
-    dkv_on(IMG - 1)
     early = r.early
     early[...] = jnp.zeros_like(early)
     early[0:48, 0:128] = rel[0:48]
     early[0:48, 128:256] = rel[48:96]
     early[0:32, 256:384] = rel[96:128]
-    for i, piece in enumerate((acc[0:1, 2 * D : 3 * D], acc[0:1, 3 * D :], acc[1:2, 0:D], acc[1:2, D : 2 * D])):
-        early[48 + i : 49 + i, D:] = piece
-    early[58:59, :] = acc[2:3, : 2 * D]
-    early[59:60, :] = acc[2:3, 2 * D :]
+    early[48:49, :] = acc[0:1, 2 * D :]
+    early[49:50, :] = acc[1:2, 0 : 2 * D]
+    early[50:51, :] = acc[2:3, : 2 * D]
+    early[51:52, :] = acc[2:3, 2 * D :]
+    for k in range(HG):
+        r.sp[0][k] = early[16 * k : 16 * (k + 1), :]
+    small_stage_one(0)
 
     has_above = (hh > 0).astype(f32)
     has_below = (hh < HG - 1).astype(f32)
-    back_up.wait_recv()
-    back_down.wait_recv()
 
     def queries_back(n):
+        halo_back(n, 0, below).wait_recv()
+        halo_back(n, 1, above).wait_recv()
         edge = jnp.concatenate([r.dqr[0, n].astype(f32) * has_above, r.dqr[1, n].astype(f32) * has_below], axis=0)
         edge = nn(r.spread[:, : 2 * HX], edge.astype(bf16))
         nothing = jnp.zeros((R, D), f32)
@@ -666,18 +725,6 @@
                 total = total + poolq[3 * a + b : 3 * a + b + 1, :] * here
                 paccq[3 * a + b] += folded(here * own)
         r.pq[n] = (total * cell_mask(n)).astype(bf16)
-
-    loop(0, IMG, queries_back)
-    r.f_q[...] = tn(flat(r.ne), flat(r.pq))
-    for b in range(B):
-        r.d[2][b] = r.f_q[rows * b : rows * (b + 1), :].astype(bf16)
-    stage_one(2)
-    for t in range(9):
-        early[48 + t : 49 + t, 0:D] = jnp.sum(paccq[t], axis=0, keepdims=True)
-    early[57:58, 0:D] = nn(ones, flat(r.pq))[0:1]
-    for k in range(2):
-        r.sp[0][k] = early[32 * k : 32 * (k + 1), :]
-    small_stage_one(0)
 
     def keys_values_back(n):
         dkv_one(n, 1, hh, hh).wait_recv()
@@ -699,36 +746,46 @@
         result = jnp.concatenate(pairs, axis=1).reshape(T, 2 * D)
         r.pkv[n] = (result * cell_mask(n)).astype(bf16)
 
-    loop(0, IMG, keys_values_back)
+    keys_values_back(0)
+    for n in range(IMG):
+        queries_back(n)
+    r.f_q[...] = tn(flat(r.ne), flat(r.pq))
+    for b in range(B):
+        r.d[2][b] = r.f_q[rows * b : rows * (b + 1), :].astype(bf16)
+    stage_one(2)
+    keys_values_back(1)
+    small_stage_two(0)
+    for n in range(IMG):
+        r.gq[n] = nt(r.pq[n], wq[...])
+    stage_two(2)
+    keys_values_back(2)
 
     r.f_kv[...] = tn(flat(r.ne), flat(r.pkv))
     for b in range(B):
         r.d[0][b] = r.f_kv[rows * b : rows * (b + 1), :].astype(bf16)
     stage_one(0)
-    stage_two(2)
-    small_stage_two(0)
 
     def projection_back(n):
-        grad = nt(r.pq[n], wq[...]) + nt(r.pkv[n], wkv[...])
+        grad = r.gq[n] + nt(r.pkv[n], wkv[...])
         hat = r.hat_one[n]
         acc[0:1, 0:D] += jnp.sum(grad * hat, axis=0, keepdims=True)
         acc[0:1, D : 2 * D] += jnp.sum(grad, axis=0, keepdims=True)
         r.v_ig[n] = r.mgd[n] + normalise_back(grad, gain_one, hat, r.inv_one[n])
 
-        @pl.when(n == 0)
-        def _():
-            stage_two(0)
-
-    loop(0, IMG, projection_back)
+    projection_back(0)
+    projection_back(1)
+    stage_two(0)
+    projection_back(2)
     input_out = pltpu.make_async_copy(r.v_ig, r.o_ig, r.s_out.at[1])
     input_out.start()
 
     late = r.late
-    late[...] = jnp.zeros_like(late)
     for t in range(9):
         late[t : t + 1, :] = jnp.sum(pacckv[t], axis=0, keepdims=True)
+        late[11 + t // 2 : 12 + t // 2, D * (t % 2) : D * (t % 2 + 1)] = jnp.sum(paccq[t], axis=0, keepdims=True)
     late[9:10, :] = nn(ones, flat(r.pkv))[0:1]
     late[10:11, :] = acc[0:1, 0 : 2 * D]
+    late[15:16, D:] = nn(ones, flat(r.pq))[0:1]
     for k in range(2):
         r.sp[1][k] = late[8 * k : 8 * (k + 1), :]
     small_stage_one(1)
@@ -742,16 +799,13 @@
         stage_four(i)
     for j in range(2):
         small_stage_four(j)
-    outs = list(zip(r.z, r.o_z)) + list(zip(r.sz, r.o_sz))
-    outs = [pltpu.make_async_copy(a, b, r.s_out.at[2 + k]) for k, (a, b) in enumerate(outs)]
-    for out in outs:
-        out.start()
-
-    for copy in (halo_up, halo_down, back_up, back_down, rest_handed(side, twin)):
+
+    for copy in (halo_up, halo_down, in_handed(side, twin), rest_handed(side, twin)):
         copy.wait_send()
 
     def sent_weights(k):
-        in_copy(k).wait_send()
+        in_copy(0, k).wait_send()
+        in_copy(1, k).wait_send()
         rest_copy(k).wait_send()
         for j in range(2):
             small_two(j, k).wait_send()
@@ -765,12 +819,15 @@
         dkv_one(n, 0, corner, twin).wait_send()
         dkv_one(n, 1, twin, twin).wait_send()
         dkv_two(n, across).wait_send()
+        halo_back(n, 0, above).wait_send()
+        halo_back(n, 1, below).wait_send()
 
     loop(0, IMG, sent_images)
     for i in range(3):
         one_copy(i, 1 - side, twin).wait_send()
     for j in range(2):
-        small_one(j, 1 - side, twin).wait_send()
+        small_stage_one_sent(j)
+        small_own(j).wait()
         for k, target in enumerate(others):
             small_three(j, k, hh, target).wait_send()
 
@@ -785,13 +842,12 @@
     @pl.when(owned)
     def _():
         for i in range(3):
+            three_own(i).wait()
             for k, target in enumerate(others):
                 three_copy(i, k, pair, target).wait_send()
 
     result_out.wait()
     input_out.wait()
-    for out in outs:
-        out.wait()
 
 
 def adam_step(weight, first_state, second_state, gradient, step_rate, decay_rate):
@@ -823,24 +879,24 @@
     for i in range(5):
         arrivals[i].wait()
     planes = [x[0].astype(f32) + x[1].astype(f32) for x in r.v_given[0:3]]
-    early, late = [
-        jnp.concatenate([x[0] + x[2], x[1] + x[3]], axis=0) for x in r.v_given[3:5]
-    ]
+    early, late = r.v_given[3:5]
+    early = jnp.concatenate([early[k] for k in range(HG)], axis=0)
+    late = jnp.concatenate([late[0] + late[2], late[1] + late[3]], axis=0)
     pack = planes[1]
     rel = jnp.concatenate([early[0:48, 0:128], early[0:48, 128:256], early[0:32, 256:384]], axis=0)
     for t in range(9):
-        r.pgrad[t, 0:1, :] = early[48 + t : 49 + t, 0:D]
+        r.pgrad[t, 0:1, :] = late[11 + t // 2 : 12 + t // 2, D * (t % 2) : D * (t % 2 + 1)]
         r.pgrad[t, 1:2, :] = late[t : t + 1, 0:D]
         r.pgrad[t, 2:3, :] = late[t : t + 1, D:]
     bgrad = r.bgrad
     bgrad[0:1, 0:D] = late[10:11, D:]
-    bgrad[0:1, D : 2 * D] = early[49:50, D:]
-    bgrad[0:1, 2 * D : 3 * D] = early[57:58, 0:D]
+    bgrad[0:1, D : 2 * D] = early[48:49, D:]
+    bgrad[0:1, 2 * D : 3 * D] = late[15:16, D:]
     bgrad[0:1, 3 * D : 5 * D] = late[9:10, :]
-    bgrad[0:1, 5 * D : 6 * D] = early[50:51, D:]
-    bgrad[0:1, 6 * D : 8 * D] = early[58:59, :]
-    bgrad[0:1, 8 * D : 10 * D] = early[59:60, :]
-    bgrad[0:1, 10 * D :] = early[51:52, D:]
+    bgrad[0:1, 5 * D : 6 * D] = early[49:50, 0:D]
+    bgrad[0:1, 6 * D : 8 * D] = early[50:51, :]
+    bgrad[0:1, 8 * D : 10 * D] = early[51:52, :]
+    bgrad[0:1, 10 * D :] = early[49:50, D:]
     given = [r.v_given[5 + 3 * index : 8 + 3 * index] for index in range(9)]
     gradients = [
         lambda: jnp.concatenate([planes[2], planes[0]], axis=1),
@@ -850,7 +906,7 @@
         lambda: r.pgrad[...],
         lambda: rel[0 : given[5][0].shape[0], 0:HD],
         lambda: rel[64 : 64 + given[6][0].shape[0], 0:HD],
-        lambda: jnp.concatenate([late[10:11, 0:D], early[48:49, D:]], axis=0),
+        lambda: jnp.concatenate([late[10:11, 0:D], early[48:49, 0:D]], axis=0),
         lambda: bgrad[...],
     ]
     leaving = []
@@ -940,7 +996,7 @@
         o_res=jax.ShapeDtypeStruct((IMG, T, D), bf16),
         o_ig=jax.ShapeDtypeStruct((IMG, T, D), f32),
         o_z=[jax.ShapeDtypeStruct((2, rows, x), y) for x, y in ((2 * D, f32), (PE, bf16), (D, f32))],
-        o_sz=[jax.ShapeDtypeStruct((HG, x, 2 * D), f32) for x in (32, 8)],
+        o_sz=[jax.ShapeDtypeStruct((HG, x, 2 * D), f32) for x in (16, 8)],
     )
     lanes = (2 * D, PE, D)
     scratch = dict(
@@ -955,16 +1011,17 @@
         v_relw=vm(weights[6].shape, f32),
         v_gains=vm(weights[7].shape, f32),
         v_biases=vm((1,) + weights[8].shape, f32),
-        gin=vm((B, rows, 3 * D), bf16),
+        gkv=vm((2, B, rows, D), bf16),
+        gq_in=vm((B, rows, D), bf16),
         grest=vm((2, B, rows, PH), bf16),
         d=[vm((B, rows, x), bf16) for x in lanes],
         p=[vm((HB, rows, x), bf16) for x in lanes],
         t=[vm((HB, rows, x), bf16) for x in lanes],
         u=[vm((B, rows, x), bf16) for x in lanes],
         z=[vm(x.shape, x.dtype) for x in results["o_z"]],
-        sp=[vm((2, x, 2 * D), f32) for x in (32, 8)],
-        sr=[vm((x, 2 * D), f32) for x in (32, 8)],
-        su=[vm((B, 32, 2 * D), bf16), vm((B, 8, 2 * D), f32)],
+        sp=[vm((HG, 16, 2 * D), f32), vm((2, 8, 2 * D), f32)],
+        sr=[vm((HG - 1, 16, 2 * D), f32), vm((1, 8, 2 * D), f32)],
+        su=[vm((B, x, 2 * D), bf16) for x in (16, 8)],
         sz=[vm(x.shape, x.dtype) for x in results["o_sz"]],
         early=vm((64, 2 * D), f32),
         late=vm((16, 2 * D), f32),
@@ -1007,6 +1064,7 @@
         qh=vm((IMG, T, D), bf16),
         qa=vm((IMG, 2, T, 256), bf16),
         probs=vm((IMG, 2, KEYS, T), f32),
+        sg=vm((IMG, 2, KEYS, T), bf16),
         mxh=vm((IMG, T, D), bf16),
         sh=vm((IMG, T, D), bf16),
         ac=vm((IMG, T, HID), bf16),
@@ -1024,27 +1082,34 @@
         dqr=vm((2, IMG, HX, D), bf16),
         dr=vm((IMG, T, 512), bf16),
         pq=vm((IMG, T, D), bf16),
+        gq=vm((IMG, T, D), f32),
         pkv=vm((IMG, T, 2 * D), bf16),
         s_local=dma((11,)),
-        s_out=dma((7,)),
-        s_wsend=dma((2, B)),
-        s_wrecv=dma((3, B)),
+        s_out=dma((2,)),
+        s_isend=dma((2, B)),
+        s_irecv=dma((2, B)),
+        s_wsend=dma((B,)),
+        s_wrecv=dma((B,)),
+        s_hand=dma((4,)),
         s_hsend=dma((2,)),
         s_hrecv=dma((2,)),
         s_ksend=dma((IMG, 3)),
         s_krecv=dma((IMG, 3)),
         s_dsend=dma((IMG, 3)),
         s_drecv=dma((IMG, 3)),
-        s_qsend=dma((2,)),
-        s_qrecv=dma((2,)),
+        s_qsend=dma((IMG, 2)),
+        s_qrecv=dma((IMG, 2)),
         s_onesend=dma((3,)),
         s_onerecv=dma((3,)),
         s_twosend=dma((3, HB)),
         s_tworecv=dma((3, B)),
+        s_three=dma((3,)),
+        s_smallown=dma((2,)),
         s_threesend=dma((3, 3)),
         s_threerecv=dma((3, 2)),
-        s_smallsend=dma((2,)),
-        s_smallrecv=dma((2,)),
+        s_earlysend=dma((HG - 1,)),
+        s_earlyrecv=dma((HG - 1,)),
+        s_late=dma((2,)),
         s_smalltwo=dma((2, B)),
         s_smalltwor=dma((2, B)),
         s_smallthree=dma((2, 3)),

time: 62.7 us -> 55.2 us (0.88)
  Pallas kernels: 61.5 us -> 54.2 us
    pallas_call x2, Pallas kernels: 61.5 us -> 54.2 us  [call(): pl.pallas_call(ordered, out_shape=flat_results, in_specs=[specs.get(id(x)...]
where the time goes in v3:
time: 55.2 us; the launch traced here: 55 us
  Pallas kernels  54.2 us (98%)
  between operations  0.85 us (2%)
    pallas_call x2, Pallas kernels, call(): pl.pallas_call(ordered, out_shape=flat_results, in_specs=[specs.get(id(x)...  54.2 us

profile of v3, /device:TPU:0, one launch (start us, length us, event | category | flops | bytes accessed | tf_op | source)
XLA Modules:
  0.0 55.0 jit_solution(5679817335627091008)
XLA Ops:
  0.7 50.4 %block.1 = (f32[3,224,192]{2,1,0:T(8,128)}, bf16[3,224,192]{2,1,0:T(8,128)(2,1)}, f32[4,16,384]{2,1,0:T(8,128)}, f32[4,8,384]{2,1,0:T(8,128)}, f32[2,24,384]{2,1...) custom-call(bf16[3,224,192]{2,1,0:T(8,128)(2,1)} %bitcast.19, f32[2112]{0:T(1024)} %refs_29_.1, ...), custom_call_target="tpu_custom_call" | custom-call | tf_op jit(solution)/shard_map/block/pallas_call | solution.py:971
  51.1 3.7 %adam.1 = (f32[24,576]{1,0:T(8,128)}, f32[24,576]{1,0:T(8,128)}, f32[24,576]{1,0:T(8,128)}, bf16[24,576]{1,0:T(8,128)(2,1)}, f32[24,192]{1,0:T(8,128)}, /*index=...) custom-call(f32[2,24,384]{2,1,0:T(8,128)} %get-tuple-element.73.refs, ...), custom_call_target="tpu_custom_call" | custom-call | tf_op jit(solution)/shard_map/adam/pallas_call | solution.py:971

commit v4 on v3

--- a/solution.py
+++ b/solution.py
@@ -91,6 +91,11 @@
     corner = lax.rem(twin + 2, HG)
 
     def loop(first, last, body):
+        if last - first < 8:
+            for i in range(first, last):
+                body(i)
+            return
+
         def step(i, carry):
             body(i)
             return carry
@@ -387,9 +392,6 @@
         kv_copy(n, 1, across, hh).wait_recv()
         kv_copy(n, 2, across, twin).start()
 
-    for n in range(IMG):
-        kv_on(n)
-
     key_at = iota((KEYS, 1), 0)
     probs, mxh = r.probs, r.mxh
 
@@ -412,11 +414,14 @@
             mixed.append(nn(value[HD * hd : HD * (hd + 1)], prob.astype(bf16)))
         mxh[n] = (jnp.concatenate(mixed, axis=0).T + qp[n]).astype(bf16)
 
-    for n in range(IMG):
-        attention(n)
-        if n == 1:
-            loop(1, B, lambda k: rest_arrival(k).wait_recv())
-            rest_handed(side, twin).start()
+    kv_on(0)
+    kv_on(1)
+    attention(0)
+    kv_on(2)
+    attention(1)
+    loop(1, B, lambda k: rest_arrival(k).wait_recv())
+    rest_handed(side, twin).start()
+    attention(2)
 
     rest_handed(1 - side, hh).wait_recv()
     for b in range(B):
@@ -442,7 +447,7 @@
         activated = (expanded * half_erf).astype(bf16)
         slope = half_erf + expanded * jnp.exp(expanded * expanded * -0.5) * 0.3989422804014327
         r.ac[n] = activated
-        r.v_res[n] = (mask * (middle + nn(activated, wred[...]) + bias_red)).astype(bf16)
+        r.mid[n] = middle
         upstream = r.v_cot[n].astype(f32) * mask
         up_half = upstream.astype(bf16)
         r.uh[n] = up_half
@@ -459,8 +464,6 @@
 
     for n in range(IMG):
         feed_forward(n)
-    result_out = pltpu.make_async_copy(r.v_res, r.o_res, r.s_out.at[0])
-    result_out.start()
 
     ones = jnp.ones((16, IMG * T), bf16)
 
@@ -747,13 +750,13 @@
         r.pkv[n] = (result * cell_mask(n)).astype(bf16)
 
     keys_values_back(0)
+    keys_values_back(1)
     for n in range(IMG):
         queries_back(n)
     r.f_q[...] = tn(flat(r.ne), flat(r.pq))
     for b in range(B):
         r.d[2][b] = r.f_q[rows * b : rows * (b + 1), :].astype(bf16)
     stage_one(2)
-    keys_values_back(1)
     small_stage_two(0)
     for n in range(IMG):
         r.gq[n] = nt(r.pq[n], wq[...])
@@ -789,17 +792,19 @@
     for k in range(2):
         r.sp[1][k] = late[8 * k : 8 * (k + 1), :]
     small_stage_one(1)
+
+    def output(n):
+        r.v_res[n] = (cell_mask(n) * (r.mid[n] + nn(r.ac[n], wred[...]) + bias_red)).astype(bf16)
+
+    output(0)
+    output(1)
+    small_stage_two(1)
+    output(2)
+    result_out = pltpu.make_async_copy(r.v_res, r.o_res, r.s_out.at[0])
+    result_out.start()
     stage_three(1)
-    small_stage_two(1)
     stage_three(2)
     small_stage_three(0)
-    stage_three(0)
-    small_stage_three(1)
-    for i in (1, 2, 0):
-        stage_four(i)
-    for j in range(2):
-        small_stage_four(j)
-
     for copy in (halo_up, halo_down, in_handed(side, twin), rest_handed(side, twin)):
         copy.wait_send()
 
@@ -827,9 +832,6 @@
         one_copy(i, 1 - side, twin).wait_send()
     for j in range(2):
         small_stage_one_sent(j)
-        small_own(j).wait()
-        for k, target in enumerate(others):
-            small_three(j, k, hh, target).wait_send()
 
     def sent_two(j):
         @pl.when(side * HB + j != me)
@@ -838,6 +840,17 @@
                 two_copy(i, j, side * HB + j).wait_send()
 
     loop(0, HB, sent_two)
+
+    stage_three(0)
+    small_stage_three(1)
+    for i in (1, 2, 0):
+        stage_four(i)
+    for j in range(2):
+        small_stage_four(j)
+    for j in range(2):
+        small_own(j).wait()
+        for k, target in enumerate(others):
+            small_three(j, k, hh, target).wait_send()
 
     @pl.when(owned)
     def _():
@@ -1071,6 +1084,7 @@
         uh=vm((IMG, T, D), bf16),
         eg=vm((IMG, T, HID), bf16),
         mgd=vm((IMG, T, D), f32),
+        mid=vm((IMG, T, D), f32),
         ag=vm((IMG, T, D), bf16),
         mg=vm((IMG, T, D), bf16),
         v_res=vm((IMG, T, D), bf16),

time: 55.2 us -> 54.5 us (0.987)
  Pallas kernels: 54.2 us -> 53.4 us
    pallas_call x2, Pallas kernels: 54.2 us -> 53.4 us  [call(): pl.pallas_call(ordered, out_shape=flat_results, in_specs=[specs.get(id(x)...]
where the time goes in v4:
time: 54.5 us; the launch traced here: 54.3 us
  Pallas kernels  53.4 us (98%)
  between operations  0.85 us (2%)
    pallas_call x2, Pallas kernels, call(): pl.pallas_call(ordered, out_shape=flat_results, in_specs=[specs.get(id(x)...  53.4 us

profile of v4, /device:TPU:0, one launch (start us, length us, event | category | flops | bytes accessed | tf_op | source)
XLA Modules:
  0.0 54.3 jit_solution(3503183551199283815)
XLA Ops:
  0.7 49.7 %block.1 = (f32[3,224,192]{2,1,0:T(8,128)}, bf16[3,224,192]{2,1,0:T(8,128)(2,1)}, f32[4,16,384]{2,1,0:T(8,128)}, f32[4,8,384]{2,1,0:T(8,128)}, f32[2,24,384]{2,1...) custom-call(bf16[3,224,192]{2,1,0:T(8,128)(2,1)} %bitcast.19, f32[2112]{0:T(1024)} %refs_29_.1, ...), custom_call_target="tpu_custom_call" | custom-call | tf_op jit(solution)/shard_map/block/pallas_call | solution.py:984
  50.4 3.7 %adam.1 = (f32[24,576]{1,0:T(8,128)}, f32[24,576]{1,0:T(8,128)}, f32[24,576]{1,0:T(8,128)}, bf16[24,576]{1,0:T(8,128)(2,1)}, f32[24,192]{1,0:T(8,128)}, /*index=...) custom-call(f32[2,24,384]{2,1,0:T(8,128)} %get-tuple-element.73.refs, ...), custom_call_target="tpu_custom_call" | custom-call | tf_op jit(solution)/shard_map/adam/pallas_call | solution.py:984
